TPU v7x, 128 devices: a whole 4x4x4 slice. The times are simulated.
128 devices in a mesh: fsdp: 128 (over x, z, y, core).
Axes of the slice: x: 4, y: 4, z: 4, core: 2. Of those that a mesh axis runs over, the one named last changes fastest.
Arguments:
- tokens: bfloat16 [32768, 1024], P('fsdp'), may hold values from -6 to 6
- segments: int32 [256, 128], P('fsdp'), may hold values from -1 to 3, as said below
- grad_out: bfloat16 [32768, 1024], P('fsdp'), may hold values from -24 to 24
- ln1_gain: bfloat16 [1024], P('fsdp'), may hold values from 0.099609375 to 1.8984375
- ln1_bias: bfloat16 [1024], P('fsdp'), may hold values from -4 to 4
- ln2_gain: bfloat16 [1024], P('fsdp'), may hold values from 0.099609375 to 1.8984375
- ln2_bias: bfloat16 [1024], P('fsdp'), may hold values from -4 to 4
- w_qkv: bfloat16 [1024, 3072], P('fsdp'), may hold values from -0.1875 to 0.1875
- b_qkv: bfloat16 [3072], P('fsdp'), may hold values from -4 to 4
- w_dense: bfloat16 [1024, 1024], P('fsdp'), may hold values from -0.75 to 0.75
- b_dense: bfloat16 [1024], P('fsdp'), may hold values from -4 to 4
- w_fc1: bfloat16 [1024, 4096], P('fsdp'), may hold values from -0.1875 to 0.1875
- b_fc1: bfloat16 [4096], P('fsdp'), may hold values from -4 to 4
- w_fc2: bfloat16 [4096, 1024], P('fsdp'), may hold values from -0.09375 to 0.09375
- b_fc2: bfloat16 [1024], P('fsdp'), may hold values from -4 to 4
Outputs:
- out: bfloat16 [32768, 1024], P('fsdp')
- grad_tokens: bfloat16 [32768, 1024], P('fsdp')
- grad_ln1_gain: float32 [1024], P('fsdp')
- grad_ln1_bias: float32 [1024], P('fsdp')
- grad_ln2_gain: float32 [1024], P('fsdp')
- grad_ln2_bias: float32 [1024], P('fsdp')
- grad_w_qkv: float32 [1024, 3072], P('fsdp')
- grad_b_qkv: float32 [3072], P('fsdp')
- grad_w_dense: float32 [1024, 1024], P('fsdp')
- grad_b_dense: float32 [1024], P('fsdp')
- grad_w_fc1: float32 [1024, 4096], P('fsdp')
- grad_b_fc1: float32 [4096], P('fsdp')
- grad_w_fc2: float32 [4096, 1024], P('fsdp')
- grad_b_fc2: float32 [1024], P('fsdp')
Inputs may be any that keep to these rules, and one draw needn't show every extreme that they name: `segments`: in each block of 128 rows (one device's micro-batch) the live rows come first with segment numbers that never fall, and padding rows (-1) follow; at least 64 rows of each block are live, and some block has exactly 64; some block, drawn from the seed, holds one sequence of all 128 rows.
All inputs are finite; a program needn't handle non-finite values.
Results may differ from a plain program's by a relative error of at most 0.0096.
Values may be sent and summed in bfloat16 or wider, within the bound.
A program may use at most 192 MiB of HBM per device.

v0:
```python
import math

import jax
import jax.numpy as jnp
from jax import lax
from jax.sharding import PartitionSpec as P

HEAD_DIM = 64
ROT = 16


NORM_EPS = 1e-05
MASKED = -1e30


def layer_norm(values, norm_gain, norm_shift):
    centre = values - jnp.mean(values, -1, keepdims=True)
    spread = jnp.mean(centre * centre, -1, keepdims=True)
    return centre * lax.rsqrt(spread + NORM_EPS) * norm_gain + norm_shift


def positions_allowed(segment_row):
    row_count = segment_row.shape[0]
    order = jnp.arange(row_count, dtype=jnp.int32)
    allowed = (segment_row[:, None] == segment_row[None, :]) & (order[None, :] <= order[:, None])
    position = jnp.sum(allowed.astype(jnp.int32), 1) - 1
    return (position, allowed)


def rotate(tensor, position, rot_dims):
    half_dims = rot_dims // 2
    inverse_freq = jnp.exp(
        jnp.arange(half_dims, dtype=jnp.float32) * (-2.0 * math.log(10000.0) / rot_dims)
    )
    angles = position.astype(jnp.float32)[:, None] * inverse_freq[None, :]
    cosine = jnp.cos(angles)[:, None, :]
    sine_wave = jnp.sin(angles)[:, None, :]
    first_half = tensor[..., :half_dims]
    second_half = tensor[..., half_dims:rot_dims]
    return jnp.concatenate(
        [
            first_half * cosine - second_half * sine_wave,
            second_half * cosine + first_half * sine_wave,
            tensor[..., rot_dims:],
        ],
        -1,
    )


def gelu_exact(values):
    return jax.nn.gelu(values, approximate=False)


def dot_float(left, right):
    return jnp.dot(left, right, preferred_element_type=jnp.float32)


def forward_rows(x_rows, segment_row, weights):
    (
        gain_one,
        shift_one,
        gain_two,
        shift_two,
        w_qkv,
        b_qkv,
        w_dense,
        b_dense,
        w_fc1,
        b_fc1,
        w_fc2,
        b_fc2,
    ) = weights
    x_float = x_rows.astype(jnp.float32)
    row_count, model_width = x_float.shape
    head_count = model_width // HEAD_DIM
    shape_heads = (row_count, head_count, HEAD_DIM)
    position, allowed = positions_allowed(segment_row)
    live_rows = (segment_row >= 0).astype(jnp.float32)[:, None]
    normed_one, norm_back_one = jax.vjp(
        layer_norm, x_float, gain_one.astype(jnp.float32), shift_one.astype(jnp.float32)
    )
    normed_two, norm_back_two = jax.vjp(
        layer_norm, x_float, gain_two.astype(jnp.float32), shift_two.astype(jnp.float32)
    )
    normed_one = normed_one.astype(jnp.bfloat16)
    normed_two = normed_two.astype(jnp.bfloat16)
    joined_qkv = dot_float(normed_one, w_qkv) + b_qkv.astype(jnp.float32)
    query_rot, rotate_back = jax.vjp(
        lambda tensor: rotate(tensor, position, ROT),
        joined_qkv[:, :model_width].reshape(shape_heads),
    )
    key_rot = rotate(
        joined_qkv[:, model_width : 2 * model_width].reshape(shape_heads), position, ROT
    )
    queries = query_rot.astype(jnp.bfloat16)
    keys_low = key_rot.astype(jnp.bfloat16)
    values_low = joined_qkv[:, 2 * model_width :].reshape(shape_heads).astype(jnp.bfloat16)
    scores = jnp.einsum(
        "qhd,khd->hqk", queries, keys_low, preferred_element_type=jnp.float32
    ) * HEAD_DIM ** (-0.5)
    scores = jnp.where(allowed[None], scores, MASKED)
    exp_scores = jnp.exp(scores - jnp.max(scores, -1, keepdims=True))
    attn_probs = exp_scores / jnp.sum(exp_scores, -1, keepdims=True)
    probs_low = attn_probs.astype(jnp.bfloat16)
    context = jnp.einsum("hqk,khd->qhd", probs_low, values_low, preferred_element_type=jnp.float32)
    context = context.reshape(row_count, model_width).astype(jnp.bfloat16)
    attention = dot_float(context, w_dense) + b_dense.astype(jnp.float32)
    hidden = dot_float(normed_two, w_fc1) + b_fc1.astype(jnp.float32)
    active, gelu_back = jax.vjp(gelu_exact, hidden)
    active = active.astype(jnp.bfloat16)
    feed_out = dot_float(active, w_fc2) + b_fc2.astype(jnp.float32)
    out_rows = (x_float + live_rows * (attention + feed_out)).astype(jnp.bfloat16)
    saved = (
        live_rows,
        norm_back_one,
        norm_back_two,
        normed_one,
        normed_two,
        rotate_back,
        queries,
        keys_low,
        values_low,
        attn_probs,
        probs_low,
        context,
        active,
        gelu_back,
    )
    return (out_rows, saved)


def backward_rows(saved, dy_rows, weights):
    (
        live_rows,
        norm_back_one,
        norm_back_two,
        normed_one,
        normed_two,
        rotate_back,
        queries,
        keys_low,
        values_low,
        attn_probs,
        probs_low,
        context,
        active,
        gelu_back,
    ) = saved
    w_qkv, w_dense, w_fc1, w_fc2 = (weights[4], weights[6], weights[8], weights[10])
    row_count, model_width = context.shape
    head_count = model_width // HEAD_DIM
    shape_heads = (row_count, head_count, HEAD_DIM)
    scale_factor = HEAD_DIM ** (-0.5)
    dy_float = dy_rows.astype(jnp.float32)
    branch = live_rows * dy_float
    branch_low = branch.astype(jnp.bfloat16)
    column_sum = jnp.sum(branch, 0)
    grad_dense = jnp.einsum("rd,re->de", context, branch_low, preferred_element_type=jnp.float32)
    grad_fc2 = jnp.einsum("rf,re->fe", active, branch_low, preferred_element_type=jnp.float32)
    d_context = jnp.einsum(
        "re,de->rd", branch_low, w_dense, preferred_element_type=jnp.float32
    ).astype(jnp.bfloat16)
    d_active = jnp.einsum("re,fe->rf", branch_low, w_fc2, preferred_element_type=jnp.float32)
    d_hidden = gelu_back(d_active)[0]
    grad_fc1_bias = jnp.sum(d_hidden, 0)
    d_hidden_low = d_hidden.astype(jnp.bfloat16)
    grad_fc1 = jnp.einsum("rd,rf->df", normed_two, d_hidden_low, preferred_element_type=jnp.float32)
    d_normed_two = jnp.einsum("rf,df->rd", d_hidden_low, w_fc1, preferred_element_type=jnp.float32)
    context_heads = d_context.reshape(shape_heads)
    d_probs = jnp.einsum(
        "qhd,khd->hqk", context_heads, values_low, preferred_element_type=jnp.float32
    )
    d_values = jnp.einsum(
        "hqk,qhd->khd", probs_low, context_heads, preferred_element_type=jnp.float32
    )
    d_scores = attn_probs * (d_probs - jnp.sum(attn_probs * d_probs, -1, keepdims=True))
    d_scores_low = d_scores.astype(jnp.bfloat16)
    d_queries = (
        jnp.einsum("hqk,khd->qhd", d_scores_low, keys_low, preferred_element_type=jnp.float32)
        * scale_factor
    )
    d_keys = (
        jnp.einsum("hqk,qhd->khd", d_scores_low, queries, preferred_element_type=jnp.float32)
        * scale_factor
    )
    d_query_raw = rotate_back(d_queries)[0]
    d_key_raw = rotate_back(d_keys)[0]
    d_joined = jnp.concatenate(
        [
            d_query_raw.reshape(row_count, model_width),
            d_key_raw.reshape(row_count, model_width),
            d_values.reshape(row_count, model_width),
        ],
        1,
    )
    grad_qkv_bias = jnp.sum(d_joined, 0)
    d_joined_low = d_joined.astype(jnp.bfloat16)
    grad_qkv = jnp.einsum("rd,re->de", normed_one, d_joined_low, preferred_element_type=jnp.float32)
    d_normed_one = jnp.einsum("re,de->rd", d_joined_low, w_qkv, preferred_element_type=jnp.float32)
    dx_one, grad_gain_one, grad_shift_one = norm_back_one(d_normed_one)
    dx_two, grad_gain_two, grad_shift_two = norm_back_two(d_normed_two)
    dx_rows = (dy_float + dx_one + dx_two).astype(jnp.bfloat16)
    grads = (
        grad_gain_one,
        grad_shift_one,
        grad_gain_two,
        grad_shift_two,
        grad_qkv,
        grad_qkv_bias,
        grad_dense,
        column_sum,
        grad_fc1,
        grad_fc1_bias,
        grad_fc2,
        column_sum,
    )
    return (grads, dx_rows)


def body(
    tokens,
    segments,
    grad_out,
    ln1_gain,
    ln1_bias,
    ln2_gain,
    ln2_bias,
    w_qkv,
    b_qkv,
    w_dense,
    b_dense,
    w_fc1,
    b_fc1,
    w_fc2,
    b_fc2,
):
    shards = (
        ln1_gain,
        ln1_bias,
        ln2_gain,
        ln2_bias,
        w_qkv,
        b_qkv,
        w_dense,
        b_dense,
        w_fc1,
        b_fc1,
        w_fc2,
        b_fc2,
    )
    micro_count, row_count = segments.shape
    device_count = lax.axis_size("fsdp")
    totals = tuple(
        (
            jnp.zeros((member.shape[0] * device_count,) + member.shape[1:], jnp.float32)
            for member in shards
        )
    )
    out_parts = []
    grad_parts = []
    for micro_index in range(micro_count):
        start_row = micro_index * row_count
        x_rows = tokens[start_row : start_row + row_count]
        dy_rows = grad_out[start_row : start_row + row_count]
        weights = (
            lax.all_gather(ln1_gain, "fsdp", axis=0, tiled=True),
            lax.all_gather(ln1_bias, "fsdp", axis=0, tiled=True),
            lax.all_gather(ln2_gain, "fsdp", axis=0, tiled=True),
            lax.all_gather(ln2_bias, "fsdp", axis=0, tiled=True),
            lax.all_gather(w_qkv, "fsdp", axis=0, tiled=True),
            lax.all_gather(b_qkv, "fsdp", axis=0, tiled=True),
            lax.all_gather(w_dense, "fsdp", axis=0, tiled=True),
            lax.all_gather(b_dense, "fsdp", axis=0, tiled=True),
            lax.all_gather(w_fc1, "fsdp", axis=0, tiled=True),
            lax.all_gather(b_fc1, "fsdp", axis=0, tiled=True),
            lax.all_gather(w_fc2, "fsdp", axis=0, tiled=True),
            lax.all_gather(b_fc2, "fsdp", axis=0, tiled=True),
        )
        out_rows, saved = forward_rows(x_rows, segments[micro_index], weights)
        weights = (
            lax.all_gather(ln1_gain, "fsdp", axis=0, tiled=True),
            lax.all_gather(ln1_bias, "fsdp", axis=0, tiled=True),
            lax.all_gather(ln2_gain, "fsdp", axis=0, tiled=True),
            lax.all_gather(ln2_bias, "fsdp", axis=0, tiled=True),
            lax.all_gather(w_qkv, "fsdp", axis=0, tiled=True),
            lax.all_gather(b_qkv, "fsdp", axis=0, tiled=True),
            lax.all_gather(w_dense, "fsdp", axis=0, tiled=True),
            lax.all_gather(b_dense, "fsdp", axis=0, tiled=True),
            lax.all_gather(w_fc1, "fsdp", axis=0, tiled=True),
            lax.all_gather(b_fc1, "fsdp", axis=0, tiled=True),
            lax.all_gather(w_fc2, "fsdp", axis=0, tiled=True),
            lax.all_gather(b_fc2, "fsdp", axis=0, tiled=True),
        )
        grad_list, dx_rows = backward_rows(saved, dy_rows, weights)
        totals = tuple((left + right for left, right in zip(totals, grad_list)))
        out_parts.append(out_rows)
        grad_parts.append(dx_rows)
    totals = (
        lax.psum_scatter(totals[0], "fsdp", scatter_dimension=0, tiled=True),
        lax.psum_scatter(totals[1], "fsdp", scatter_dimension=0, tiled=True),
        lax.psum_scatter(totals[2], "fsdp", scatter_dimension=0, tiled=True),
        lax.psum_scatter(totals[3], "fsdp", scatter_dimension=0, tiled=True),
        lax.psum_scatter(totals[4], "fsdp", scatter_dimension=0, tiled=True),
        lax.psum_scatter(totals[5], "fsdp", scatter_dimension=0, tiled=True),
        lax.psum_scatter(totals[6], "fsdp", scatter_dimension=0, tiled=True),
        lax.psum_scatter(totals[7], "fsdp", scatter_dimension=0, tiled=True),
        lax.psum_scatter(totals[8], "fsdp", scatter_dimension=0, tiled=True),
        lax.psum_scatter(totals[9], "fsdp", scatter_dimension=0, tiled=True),
        lax.psum_scatter(totals[10], "fsdp", scatter_dimension=0, tiled=True),
        lax.psum_scatter(totals[11], "fsdp", scatter_dimension=0, tiled=True),
    )
    return (
        jnp.concatenate(out_parts, 0),
        jnp.concatenate(grad_parts, 0),
        totals[0],
        totals[1],
        totals[2],
        totals[3],
        totals[4],
        totals[5],
        totals[6],
        totals[7],
        totals[8],
        totals[9],
        totals[10],
        totals[11],
    )


def solution(mesh):
    return jax.shard_map(
        body,
        mesh=mesh,
        in_specs=(
            P("fsdp", None),
            P("fsdp", None),
            P("fsdp", None),
            P("fsdp"),
            P("fsdp"),
            P("fsdp"),
            P("fsdp"),
            P("fsdp", None),
            P("fsdp"),
            P("fsdp", None),
            P("fsdp"),
            P("fsdp", None),
            P("fsdp"),
            P("fsdp", None),
            P("fsdp"),
        ),
        out_specs=(
            P("fsdp", None),
            P("fsdp", None),
            P("fsdp"),
            P("fsdp"),
            P("fsdp"),
            P("fsdp"),
            P("fsdp", None),
            P("fsdp"),
            P("fsdp", None),
            P("fsdp"),
            P("fsdp", None),
            P("fsdp"),
            P("fsdp", None),
            P("fsdp"),
        ),
        check_vma=False,
    )
```

profile of v0, /device:TPU:1, one launch (start us, length us, event | category | flops | bytes accessed | tf_op | source)
XLA Modules:
  0.0 2482.8 jit_solution(8007862108379746647)
XLA Ops:
  10.0 0.8 dynamic-update-slice
  11.7 0.8 dynamic-update-slice.7
  15.1 0.8 dynamic-update-slice.2
  15.9 0.8 dynamic-update-slice.6
  16.8 70.3 %all-reduce.28 = (bf16[4096]{0:T(1024)(128)(2,1)}, bf16[1024]{0:T(1024)(128)(2,1)}, bf16[1024]{0:T(1024)(128)(2,1)}, bf16[1024]{0:T(1024)(128)(2,1)}, bf16[3072]...) all-reduce(bf16[4096]{0:T(1024)(128)(2,1)S(1)} %dynamic-update-slic, ...), channel_id=1, replica_groups=mesh['fsdp'=128] {'fsdp'}, use_global_device_ids=true, to_apply=%add.18 | all-reduce | flops 13312 | bytes 53248
  88.0 1.2 convert_reduce_fusion.1
  89.2 1.3 fusion.76
  91.0 1.3 compare_convert_fusion.1
  93.7 4.0 convolution_add_fusion.5
  98.0 0.8 copy.77
  100.5 3.9 convolution_add_fusion.6
  104.7 0.8 copy.73
  105.8 1.4 subtract_convert_fusion.1
  107.2 1.4 subtract_convert_fusion.3
  108.6 1.6 fusion.154
  110.3 2.1 fusion.155
  114.8 2.8 convolution_add_fusion.7
  117.8 31.5 %all-gather.7.cloned.1.call-done = bf16[1024,1024]{1,0:T(8,128)(2,1)} async-done(((bf16[8,1024]{1,0:T(8,128)(2,1)}), bf16[1024,1024]{1,0:T(8,128)(2,1)}) %all-gather.7.cloned.1.call-update) | async-done | bytes 2097168 | tf_op jit(solution)/shard_map/all_gather | solution.py:272
  149.3 2.6 convolution_convert_fusion.1
  151.9 0.8 copy.81
  152.7 0.8 convolution_convert_fusion
  153.6 0.8 copy.85
  154.4 1.8 multiply_reduce_fusion
  163.2 2.0 fusion.115
  165.2 6.4 convolution_add_fusion.2
  172.3 47.6 %all-gather.9.cloned.1.call-done = bf16[1024,4096]{1,0:T(8,128)(2,1)} async-done(((bf16[8,4096]{1,0:T(8,128)(2,1)}), bf16[1024,4096]{1,0:T(8,128)(2,1)}) %all-gather.9.cloned.1.call-update) | async-done | bytes 8388624 | tf_op jit(solution)/shard_map/all_gather | solution.py:274
  219.9 9.7 multiply_convert_fusion.1
  229.6 60.8 %all-gather.11.cloned.1.call-done = bf16[4096,1024]{1,0:T(8,128)(2,1)} async-done(((bf16[32,1024]{1,0:T(8,128)(2,1)}), bf16[4096,1024]{1,0:T(8,128)(2,1)}) %all-gather.11.cloned.1.call-update) | async-done | bytes 8388624 | tf_op jit(solution)/shard_map/all_gather | solution.py:276
  290.4 8.0 fusion.156
  298.4 2.5 fusion.85
  300.9 9.4 multiply_convert_fusion
  310.3 8.4 fusion.157
  318.7 9.5 convolution_add_fusion.1
  328.4 3.6 fusion.141
  332.0 9.4 convolution_add_fusion
  342.1 1.8 fusion.32
  344.0 1.8 fusion.34
  345.9 5.2 fusion.120
  351.2 5.3 fusion.77
  356.6 3.0 fusion.83
  359.6 4.0 fusion.78
  364.8 64.3 %all-reduce.27 = (f32[1024]{0:T(1024)S(1)}, f32[1024]{0:T(1024)S(1)}, f32[1024]{0:T(1024)S(1)}, f32[1024]{0:T(1024)S(1)}, f32[3072]{0:T(1024)S(1)}, /*index=5*/f32[1024]{0:T(1024)S(1)}, f32[4096]{0:T(1024)S(1)}) all-reduce(f32[1024]{0:T(1024)S(1)} %add.269, f32[1024]{0:T(1024)S(1)} %add.270, ...), channel_id=2, replica_groups=mesh['fsdp'=128] {'fsdp'}, use_global_device_ids=true, to_apply=%region_22.23.clone | all-reduce | flops 12288 | bytes 98304
  432.6 5.0 convolution_add_fusion.10
  438.9 4.8 convolution_add_fusion.11
  446.3 479.9 %reduce-scatter.7.cloned.1.call-done = f32[8,1024]{1,0:T(8,128)} async-done(((f32[1024,1024]{1,0:T(8,128)}), f32[8,1024]{1,0:T(8,128)}) %reduce-scatter.7.cloned.1.call-update) | async-done | bytes 32784 | tf_op jit(solution)/shard_map/reduce_scatter | solution.py:305
  926.2 226.6 %reduce-scatter.5.cloned.1.call-done = f32[8,3072]{1,0:T(8,128)} async-done(((f32[1024,3072]{1,0:T(8,128)}), f32[8,3072]{1,0:T(8,128)}) %reduce-scatter.5.cloned.1.call-update) | async-done | bytes 98320 | tf_op jit(solution)/shard_map/reduce_scatter | solution.py:303
  1152.7 660.6 %reduce-scatter.9.cloned.1.call-done = f32[8,4096]{1,0:T(8,128)} async-done(((f32[1024,4096]{1,0:T(8,128)}), f32[8,4096]{1,0:T(8,128)}) %reduce-scatter.9.cloned.1.call-update) | async-done | bytes 131088 | tf_op jit(solution)/shard_map/reduce_scatter | solution.py:307
  1813.3 661.9 %reduce-scatter.11.cloned.1.call-done = f32[32,1024]{1,0:T(8,128)} async-done(((f32[4096,1024]{1,0:T(8,128)}), f32[32,1024]{1,0:T(8,128)}) %reduce-scatter.11.cloned.1.call-update) | async-done | bytes 131088 | tf_op jit(solution)/shard_map/reduce_scatter | solution.py:309
  (272 shorter events, 31.1 us)
Async XLA Ops:
  7.2 86.5 %all-gather.5.cloned.1.call-start = ((), (), s32[]{:S(2)}) async-start(), calls=%async_computation.4 | async-start | bytes 6340608 | tf_op jit(solution)/shard_map/all_gather | solution.py:270
  7.9 141.4 %all-gather.7.cloned.1.call-start = ((), (), s32[]{:S(2)}) async-start(), calls=%async_computation.5 | async-start | bytes 2113536 | tf_op jit(solution)/shard_map/all_gather | solution.py:272
  8.7 211.2 %all-gather.9.cloned.1.call-start = ((), (), s32[]{:S(2)}) async-start(), calls=%async_computation.6 | async-start | bytes 8454144 | tf_op jit(solution)/shard_map/all_gather | solution.py:274
  9.4 281.0 %all-gather.11.cloned.1.call-start = ((), (), s32[]{:S(2)}) async-start(), calls=%async_computation.7 | async-start | bytes 8454144 | tf_op jit(solution)/shard_map/all_gather | solution.py:276
  10.0 916.2 %reduce-scatter.7.cloned.1.call-start = ((), (), s32[]{:S(2)}) async-start(), calls=%async_computation.9 | async-start | bytes 4227072 | tf_op jit(solution)/shard_map/reduce_scatter | solution.py:305
  90.5 7.2 copy-start.72
  91.0 9.5 copy-start.60
  91.0 6.7 copy-start.58
  97.8 2.7 copy-start
  105.6 4.7 copy-start.33
  105.8 6.5 copy-start.31
  108.6 1.7 copy-start.44
  108.6 1.7 copy-start.46
  108.6 1.7 copy-start.48
  110.2 2.2 copy-start.64
  110.2 2.4 copy-start.27
  110.2 2.1 copy-start.40
  112.7 2.1 copy-start.25
  117.6 1035.1 %reduce-scatter.5.cloned.1.call-start = ((), (), s32[]{:S(2)}) async-start(), calls=%async_computation.8 | async-start | bytes 12681216 | tf_op jit(solution)/shard_map/reduce_scatter | solution.py:303
  149.3 3.5 copy-start.1
  151.9 2.6 copy-start.65
  154.4 1.9 copy-start.28
  160.9 4.3 copy-start.3
  161.1 4.0 copy-start.5
  161.2 1.8 copy-start.10
  162.5 2.7 copy-start.8
  163.0 2.2 copy-start.17
  163.2 2.0 copy-start.59
  171.6 1641.7 %reduce-scatter.9.cloned.1.call-start = ((), (), s32[]{:S(2)}) async-start(), calls=%async_computation.10 | async-start | bytes 16908288 | tf_op jit(solution)/shard_map/reduce_scatter | solution.py:307
  298.4 2.5 copy-start.21
  328.2 2147.0 %reduce-scatter.11.cloned.1.call-start = ((), (), s32[]{:S(2)}) async-start(), calls=%async_computation.11 | async-start | bytes 16908288 | tf_op jit(solution)/shard_map/reduce_scatter | solution.py:309
  341.5 4.3 copy-start.4
  341.5 4.3 copy-start.6
  341.5 4.3 copy-start.9
  345.9 5.2 copy-start.11
  345.9 5.2 copy-start.13
  345.9 5.2 copy-start.18
  345.9 10.6 slice-start
  351.1 8.5 copy-start.19
  351.1 5.3 copy-start.75
  351.1 5.4 copy-start.73
  351.1 5.4 slice-start.1
  351.2 5.4 copy-start.16
  356.6 3.0 copy-start.22
  359.6 4.1 copy-start.14
  429.7 2045.5 %copy-start.76 = (f32[8]{0:T(128)}, f32[8]{0:T(128)S(1)}, u32[]{:S(2)}) copy-start(f32[8]{0:T(128)S(1)} %dynamic-slice.5) | copy-start | bytes 100
  432.6 5.0 copy-start.26
  438.9 4.8 copy-start.24
  (40 other events, 42.7 us)
Sparse Core Ops, SparseCore 0:
  11.1 71.9 all-gather.4
  86.3 62.9 all-gather.6
  152.3 67.5 all-gather.8
  222.7 67.6 all-gather.10
  293.2 632.9 reduce-scatter.6
  932.3 220.3 reduce-scatter.4
  1155.8 657.4 reduce-scatter.8
  1816.4 658.7 reduce-scatter.10
where the time goes:
time: 2500 us; the launch traced here: 2480 us
  waiting for transfers between devices  2170 us (87%)
  blocking collectives  135 us (5%)
  matrix products  121 us (5%)
    reduce_scatter x1, waiting for transfers between devices, body(): lax.psum_scatter(totals[10], 'fsdp', scatter_dimension=0, tiled=True)  662 us
    reduce_scatter x1, waiting for transfers between devices, body(): lax.psum_scatter(totals[8], 'fsdp', scatter_dimension=0, tiled=True)  661 us
    reduce_scatter x1, waiting for transfers between devices, body(): lax.psum_scatter(totals[6], 'fsdp', scatter_dimension=0, tiled=True)  480 us
    reduce_scatter x1, waiting for transfers between devices, body(): lax.psum_scatter(totals[4], 'fsdp', scatter_dimension=0, tiled=True)  227 us
    unnamed x2, blocking collectives  135 us
    all_gather x1, waiting for transfers between devices, body(): lax.all_gather(w_fc2, 'fsdp', axis=0, tiled=True)  60.8 us
  transfers between devices with their start and end apart: 8, of which 7 were waited for; matrix products, arithmetic and copies ran while one was open for 6% of the time, Pallas kernels for 0%

commit v1 on v0

v1 whole, which is shorter than its diff:
```python
import functools
import math

import jax
import jax.numpy as jnp
import numpy as np
from jax import lax
from jax.experimental import pallas as pl
from jax.experimental.pallas import tpu as pltpu
from jax.sharding import PartitionSpec as P

NORM_EPS = 1e-05
MASKED = -1e30
MESH = pl.DeviceIdType.MESH
BF = jnp.bfloat16
F32 = jnp.float32
VMEM_LIMIT = 60 * 1024 * 1024


def coords():
    i = lax.axis_index("fsdp")
    core = lax.rem(i, 2)
    y = lax.rem(i // 2, 4)
    z = lax.rem(i // 8, 4)
    x = i // 32
    return x, z, y, core


def ident(x, z, y, core):
    return ((x * 4 + z) * 4 + y) * 2 + core


class Ring:
    def __init__(self, at, core):
        step = 1 + 2 * core
        self.own = at
        self.fwd = lax.rem(at + step, 4)
        self.bwd = lax.rem(at + 4 - step, 4)
        self.opp = lax.rem(at + 2, 4)


class Messages:
    def __init__(self, send_sem, recv_sem):
        self.send_sem, self.recv_sem = send_sem, recv_sem
        self.sent, self.landed = {}, set()

    def send(self, name, src, dst, target):
        n = len(self.sent)
        copy = pltpu.make_async_remote_copy(
            src_ref=src,
            dst_ref=dst,
            send_sem=self.send_sem.at[n],
            recv_sem=self.recv_sem.at[n],
            device_id=(target,),
            device_id_type=MESH,
        )
        copy.start()
        self.sent[name] = copy

    def land(self, name):
        assert name not in self.landed
        self.landed.add(name)
        self.sent[name].wait_recv()

    def finish(self):
        for name, copy in self.sent.items():
            if name not in self.landed:
                copy.wait_recv()
        for copy in self.sent.values():
            copy.wait_send()


def enter(targets):
    barrier = pltpu.get_barrier_semaphore()
    for target in targets:
        pl.semaphore_signal(barrier, inc=1, device_id=(target,), device_id_type=MESH)
    pl.semaphore_wait(barrier, len(targets))


def group_member(x, z, t):
    return ident(x, z, 0, 0) + t


GATHER_MESSAGES = 7 + 7 + 2 * 7 + 2 * (3 + 12)
PARTS = (("a", 0, 7), ("b", 7, 13))


def gather_kernel(x_ref, dy_ref, seg_ref, wl_ref, rest_ref, X, DY, SEG, WB, send_sem, recv_sem, local_sem):
    x, z, y, core = coords()
    t = y * 2 + core
    ring_y, ring_x, ring_z = Ring(y, core), Ring(x, core), Ring(z, core)
    y_dev = lambda to: ident(x, z, to, core)
    x_dev = lambda to: ident(to, z, y, core)
    z_dev = lambda to: ident(x, to, y, core)
    sibling = ident(x, z, y, 1 - core)
    others = [lax.rem(t + k, 8) for k in range(1, 8)]

    enter(
        [group_member(x, z, o) for o in others]
        + [x_dev(ring_x.fwd), x_dev(ring_x.bwd), z_dev(ring_z.fwd), z_dev(ring_z.bwd)]
    )
    msgs = Messages(send_sem, recv_sem)

    local = [
        pltpu.make_async_copy(wl_ref.at[t], WB.at[x, z, t], local_sem.at[0]),
        pltpu.make_async_copy(rest_ref, WB.at[x, z, pl.ds(8, 5)], local_sem.at[1]),
        pltpu.make_async_copy(x_ref, X.at[t], local_sem.at[2]),
        pltpu.make_async_copy(dy_ref, DY.at[t], local_sem.at[3]),
        pltpu.make_async_copy(seg_ref, SEG.at[t], local_sem.at[4]),
    ]
    for copy in local:
        copy.start()
    for k, o in enumerate(others):
        msgs.send(("w", k), wl_ref.at[o], WB.at[x, z, t], group_member(x, z, o))
    rows = (("x", x_ref, X), ("d", dy_ref, DY))

    def own_rows(name, src, dst):
        msgs.send((name, 0), src, dst.at[t], y_dev(ring_y.fwd))
        msgs.send((name, 1), src, dst.at[t], y_dev(ring_y.bwd))
        msgs.send((name, 2), src, dst.at[t], sibling)

    own_rows(*rows[0])
    for k, o in enumerate(others):
        msgs.send(("s", k), seg_ref, SEG.at[t], group_member(x, z, o))
    own_rows(*rows[1])
    for copy in local:
        copy.wait()
    for k in range(7):
        msgs.land(("w", k))

    def piece(half, p, q):
        name, lo, hi = half
        if name == "a":
            return WB.at[p, q, pl.ds(lo, hi - lo)]
        return WB.at[q, p, pl.ds(lo, hi - lo)]

    def axes(half):
        if half[0] == "a":
            return ring_x, x_dev, ring_z, z_dev
        return ring_z, z_dev, ring_x, x_dev

    def first(half, k, at, to):
        one, one_dev, two, _ = axes(half)
        ref = piece(half, at, two.own)
        msgs.send((half[0], "p", k), ref, ref, one_dev(to))

    def second(half, sub, k, at, frm, to):
        _, _, two, two_dev = axes(half)
        ref = piece(half, at, frm)
        msgs.send((half[0], sub, k), ref, ref, two_dev(to))

    def spread(half, sub, at):
        two = axes(half)[2]
        second(half, sub, 0, at, two.own, two.fwd)
        second(half, sub, 1, at, two.own, two.bwd)

    def pass_on(half, sub):
        one, _, two, _ = axes(half)
        msgs.land((half[0], sub, 0))
        second(half, sub, 2, getattr(one, sub), two.bwd, two.fwd)

    for half in PARTS:
        one = axes(half)[0]
        first(half, 0, one.own, one.fwd)
        first(half, 1, one.own, one.bwd)
        spread(half, "own", one.own)
    for half in PARTS:
        one = axes(half)[0]
        msgs.land((half[0], "p", 0))
        first(half, 2, one.bwd, one.fwd)
        spread(half, "bwd", one.bwd)
    for half in PARTS:
        msgs.land((half[0], "p", 1))
        spread(half, "fwd", axes(half)[0].fwd)
    for half in PARTS:
        msgs.land((half[0], "p", 2))
        spread(half, "opp", axes(half)[0].opp)
    for half in PARTS:
        pass_on(half, "own")

    slot = lambda at: at * 2 + core

    def rows_on(name, dst):
        msgs.land((name, 0))
        ref = dst.at[slot(ring_y.bwd)]
        msgs.send((name, 3), ref, ref, y_dev(ring_y.fwd))
        msgs.send((name, 4), ref, ref, sibling)
        msgs.land((name, 1))
        ref = dst.at[slot(ring_y.fwd)]
        msgs.send((name, 5), ref, ref, sibling)

    def rows_last(name, dst):
        msgs.land((name, 3))
        ref = dst.at[slot(ring_y.opp)]
        msgs.send((name, 6), ref, ref, sibling)

    rows_on("x", X)
    for sub in ("bwd", "fwd", "opp"):
        for half in PARTS:
            pass_on(half, sub)
    rows_on("d", DY)
    rows_last("x", X)
    rows_last("d", DY)
    msgs.finish()


def gather(x, dy, seg, wl, rest):
    any_spec = pl.BlockSpec(memory_space=pl.ANY)
    return pl.pallas_call(
        gather_kernel,
        out_shape=(
            jax.ShapeDtypeStruct((8, 256, 1024), BF),
            jax.ShapeDtypeStruct((8, 256, 1024), BF),
            jax.ShapeDtypeStruct((8, 2, 128), jnp.int32),
            jax.ShapeDtypeStruct((4, 4, 13, 8, 1024), BF),
        ),
        in_specs=[any_spec] * 5,
        out_specs=(any_spec,) * 4,
        scratch_shapes=[
            pltpu.SemaphoreType.DMA((GATHER_MESSAGES,)),
            pltpu.SemaphoreType.DMA((GATHER_MESSAGES,)),
            pltpu.SemaphoreType.DMA((5,)),
        ],
        compiler_params=pltpu.CompilerParams(collective_id=0, has_side_effects=True),
        name="gather_rows_and_weights",
    )(x, dy, seg, wl, rest)


def dot(a, b):
    return jnp.dot(a, b, preferred_element_type=F32)


def dot_nt(a, b):
    return lax.dot_general(a, b, (((1,), (1,)), ((), ())), preferred_element_type=F32)


def dot_tn(a, b):
    return lax.dot_general(a, b, (((0,), (0,)), ((), ())), preferred_element_type=F32)


def turn(u, cosine, sine, low_lanes):
    moved = jnp.where(low_lanes, pltpu.roll(u, 120, 1), pltpu.roll(u, 8, 1))
    return u * cosine + moved * sine


def block_kernel(x_ref, dy_ref, seg_ref, w1_ref, w2_ref, ln_ref, bias_ref, table_ref,
                 out_ref, g_ref, grad_ref, sum_ref, acc_n, acc_c, acc_s):
    step = pl.program_id(0)
    first, last = step == 0, step == pl.num_programs(0) - 1

    @pl.when(first)
    def _():
        acc_n[...] = jnp.zeros_like(acc_n)
        acc_c[...] = jnp.zeros_like(acc_c)
        acc_s[...] = jnp.zeros_like(acc_s)

    x = x_ref[0].astype(F32)
    centre = x - jnp.mean(x, 1, keepdims=True)
    spread = jnp.mean(centre * centre, 1, keepdims=True)
    normed = centre * lax.rsqrt(spread + NORM_EPS)
    g1, g2 = ln_ref[0:1, :], ln_ref[2:3, :]
    a1 = (normed * g1 + ln_ref[1:2, :]).astype(BF)
    a2 = (normed * g2 + ln_ref[3:4, :]).astype(BF)
    normed_b = normed.astype(BF)
    joined = dot(a1, w1_ref[:, 0:384]) + bias_ref[:, 0:384]
    hidden = dot(a2, w1_ref[:, 384:896]) + bias_ref[:, 384:896]
    phi_cdf = 0.5 + 0.5 * lax.erf(hidden * math.sqrt(0.5))
    active = (hidden * phi_cdf).astype(BF)
    slope = phi_cdf + hidden * (jnp.exp(hidden * hidden * -0.5) * (1.0 / math.sqrt(2.0 * math.pi)))

    row = lax.broadcasted_iota(jnp.int32, (128, 128), 0)
    col = lax.broadcasted_iota(jnp.int32, (128, 128), 1)
    masks, lives, tables = [], [], []
    for b in range(2):
        seg_c = jnp.broadcast_to(seg_ref[0, b : b + 1, :].astype(F32), (128, 128))
        seg_r = seg_c.T
        allowed = (seg_c == seg_r) & (col <= row)
        position = jnp.sum(allowed.astype(F32), 1, keepdims=True) - 1.0
        onehot = (col == position.astype(jnp.int32)).astype(BF)
        tables.append(dot(onehot, table_ref[...]))
        masks.append(allowed)
        lives.append((seg_r[:, 0:1] >= 0.0).astype(F32))
    dy = dy_ref[0].astype(F32) * jnp.concatenate(lives, 0)
    branch = dy.astype(BF)
    d_cat = dot_nt(branch, w2_ref[...])
    d_hidden = d_cat[:, 128:640] * slope
    d_context = d_cat[:, 0:128].astype(BF)

    lane = lax.broadcasted_iota(jnp.int32, (128, 128), 1)
    low_lanes = lax.rem(lane, 64) < 8
    head0 = lane < 64

    def stacked(u):
        zero = jnp.zeros_like(u)
        return jnp.concatenate([jnp.where(head0, u, zero), jnp.where(head0, zero, u)], 0)

    contexts, d_joined = [], []
    for b in range(2):
        part = slice(b * 128, b * 128 + 128)
        cosine = tables[b][:, 0:128] + tables[b][:, 128:256]
        sine = tables[b][:, 256:384] + tables[b][:, 384:512]
        q = turn(joined[part, 0:128], cosine, sine, low_lanes).astype(BF)
        k = turn(joined[part, 128:256], cosine, sine, low_lanes).astype(BF)
        v = joined[part, 256:384].astype(BF)
        q2 = stacked(q)
        allowed = jnp.concatenate([masks[b], masks[b]], 0)
        scores = jnp.where(allowed, dot_nt(q2, k) * 0.125, MASKED)
        e = jnp.exp(scores - jnp.max(scores, 1, keepdims=True))
        probs = e / jnp.sum(e, 1, keepdims=True)
        probs_b = probs.astype(BF)
        ctx = dot(probs_b, v)
        contexts.append(jnp.where(head0, ctx[0:128], ctx[128:256]).astype(BF))
        dc2 = stacked(d_context[part])
        d_probs = dot_nt(dc2, v)
        d_v = dot_tn(probs_b, dc2)
        d_scores = probs * (d_probs - jnp.sum(probs * d_probs, 1, keepdims=True))
        d_scores = d_scores.astype(BF)
        dq2 = dot(d_scores, k) * 0.125
        d_q = jnp.where(head0, dq2[0:128], dq2[128:256])
        d_k = dot_tn(d_scores, q2) * 0.125
        d_joined.append(
            jnp.concatenate(
                [turn(d_q, cosine, -sine, low_lanes), turn(d_k, cosine, -sine, low_lanes), d_v], 1
            )
        )
    cat = jnp.concatenate([jnp.concatenate(contexts, 0), active], 1)
    out_ref[0] = dot(cat, w2_ref[...]).astype(BF)
    acc_c[...] += dot_tn(cat, branch)
    d_all = jnp.concatenate([jnp.concatenate(d_joined, 0), d_hidden], 1)
    acc_s[0:1, 0:896] += jnp.sum(d_all, 0, keepdims=True)
    acc_s[1:2, :] += jnp.sum(dy, 0, keepdims=True)
    d_all_b = d_all.astype(BF)
    acc_n[...] += dot_tn(normed_b, d_all_b)
    g = g1 * dot_nt(d_all_b[:, 0:384], w1_ref[:, 0:384]) + g2 * dot_nt(d_all_b[:, 384:896], w1_ref[:, 384:896])
    g_ref[0] = g.astype(BF)

    @pl.when(last)
    def _():
        grad_ref[:, 0:64, 0:896] = acc_n[...].reshape(16, 64, 896).astype(BF)
        grad_ref[:, 64:96, :] = acc_c[128:640, :].reshape(16, 32, 1024).astype(BF)
        dense = acc_c[0:128, :].reshape(16, 8, 1024)
        for j in range(4):
            pair = [dense[:, :, i * 128 : i * 128 + 128] for i in (2 * j, 2 * j + 1)]
            grad_ref[:, 16 * j : 16 * j + 16, 896:1024] = jnp.concatenate(pair, 1).astype(BF)
        sum_ref[...] = acc_s[...]


def rotary_table():
    m = 8
    angle = np.arange(128, dtype=np.float64)[:, None] * (10000.0 ** (-2.0 * np.arange(m) / 16.0))[None, :]
    cosine = np.ones((128, 128), np.float32)
    sine = np.zeros((128, 128), np.float32)
    for head in (0, 64):
        cosine[:, head : head + m] = np.cos(angle)
        cosine[:, head + m : head + 2 * m] = np.cos(angle)
        sine[:, head : head + m] = -np.sin(angle)
        sine[:, head + m : head + 2 * m] = np.sin(angle)
    parts = []
    for table in (cosine, sine):
        high = table.astype(jnp.bfloat16)
        parts += [high, (table - high.astype(np.float32)).astype(jnp.bfloat16)]
    return np.concatenate(parts, 1)


def block(x, dy, seg, w1, w2, ln, bias):
    whole = lambda shape: pl.BlockSpec(shape, lambda s: (0,) * len(shape))
    rows = pl.BlockSpec((1, 256, 1024), lambda s: (s, 0, 0))
    return pl.pallas_call(
        block_kernel,
        grid=(8,),
        out_shape=(
            jax.ShapeDtypeStruct((8, 256, 1024), BF),
            jax.ShapeDtypeStruct((8, 256, 1024), BF),
            jax.ShapeDtypeStruct((16, 96, 1024), BF),
            jax.ShapeDtypeStruct((8, 1024), F32),
        ),
        in_specs=[
            rows, rows, pl.BlockSpec((1, 2, 128), lambda s: (s, 0, 0)),
            whole((1024, 1024)), whole((640, 1024)), whole((4, 1024)), whole((1, 896)), whole((128, 512)),
        ],
        out_specs=(rows, rows, whole((16, 96, 1024)), whole((8, 1024))),
        scratch_shapes=[
            pltpu.VMEM((1024, 896), F32),
            pltpu.VMEM((640, 1024), F32),
            pltpu.VMEM((8, 1024), F32),
        ],
        compiler_params=pltpu.CompilerParams(
            dimension_semantics=("arbitrary",), vmem_limit_bytes=VMEM_LIMIT
        ),
        cost_estimate=pl.CostEstimate(flops=20_000_000_000, bytes_accessed=25_000_000, transcendentals=3_000_000),
        name="block_forward_backward",
    )(x, dy, seg, w1, w2, ln, bias, jnp.asarray(rotary_table()))


def slabs(rows, step, fn):
    def one(i, carry):
        fn(pl.ds(pl.multiple_of(i * step, step), step))
        return carry

    lax.fori_loop(0, rows // step, one, 0)


SUM_MESSAGES = 3 + 3 + 7 + 2 * (4 + 3) + 2 * 6 + 7


def sum_kernel(out_ref, g_ref, blob_ref, vec_ref,
               out_sum, g_sum, all_ref, own_ref, vec_all,
               sib, held, from_y, from_one, held_one, from_two, held_two, held_last, vec_one, vec_sum, vec_two,
               send_sem, recv_sem):
    x, z, y, core = coords()
    t = y * 2 + core
    ring_y, ring_x, ring_z = Ring(y, core), Ring(x, core), Ring(z, core)
    y_dev = lambda to: ident(x, z, to, core)
    x_dev = lambda to: ident(to, z, y, core)
    z_dev = lambda to: ident(x, to, y, core)
    sibling = ident(x, z, y, 1 - core)
    others = [lax.rem(t + k, 8) for k in range(1, 8)]
    x_others = [lax.rem(x + k, 4) for k in range(1, 4)]
    z_others = [lax.rem(z + k, 4) for k in range(1, 4)]
    enter(
        [group_member(x, z, o) for o in others]
        + [x_dev(o) for o in x_others]
        + [z_dev(o) for o in z_others]
    )
    msgs = Messages(send_sem, recv_sem)
    mine = lambda at: at * 2 + core
    hers = lambda at: at * 2 + 1 - core

    arrays = ((0, out_ref, out_sum), (1, g_ref, g_sum))

    def to_sibling(a, src, role):
        at = getattr(ring_y, role)
        msgs.send(("sib", a, role), src.at[hers(at)], sib.at[a, at], sibling)

    for a, src, _ in arrays:
        to_sibling(a, src, "opp")

    def half(name):
        if name == "a":
            return ring_x, x_dev, ring_z, z_dev, (lambda p: blob_ref.at[p, :, pl.ds(0, 48)]), 0
        return ring_z, z_dev, ring_x, x_dev, (lambda p: blob_ref.at[:, p, pl.ds(48, 48)]), 1

    for k, o in enumerate(x_others):
        msgs.send(("v1", k), vec_ref, vec_one.at[k], x_dev(o))
    for name in "ab":
        one, one_dev, _, _, part, h = half(name)
        msgs.send((name, "one", 0), part(one.opp), from_one.at[h, 0], one_dev(one.fwd))
        msgs.send((name, "one", 1), part(one.bwd), from_one.at[h, 1], one_dev(one.bwd))
    for role in ("fwd", "bwd", "own"):
        for a, src, _ in arrays:
            to_sibling(a, src, role)

    def gathered(a, src, role, slot, extra=None):
        at = getattr(ring_y, role)

        def add(r):
            v = src[mine(at), r, :].astype(F32) + sib[a, at, r, :].astype(F32)
            if extra is not None:
                v = v + from_y[a, extra, r, :].astype(F32)
            held[a, slot, r, :] = v.astype(BF)

        slabs(256, 32, add)

    for a, src, _ in arrays:
        msgs.land(("sib", a, "opp"))
        gathered(a, src, "opp", 0)
        msgs.send(("y", a, 0), held.at[a, 0], from_y.at[a, 0], y_dev(ring_y.fwd))
    for a, src, _ in arrays:
        msgs.land(("sib", a, "fwd"))
        gathered(a, src, "bwd", 1)
        msgs.send(("y", a, 1), held.at[a, 1], from_y.at[a, 1], y_dev(ring_y.bwd))

    def first_forward(name):
        one, one_dev, _, _, part, h = half(name)
        msgs.land((name, "one", 0))
        block_of = part(one.fwd)

        def add(r):
            held_one[h, :, r, :] = (block_of[:, r, :].astype(F32) + from_one[h, 0, :, r, :].astype(F32)).astype(BF)

        slabs(48, 16, add)
        msgs.send((name, "one", 2), held_one.at[h], from_one.at[h, 2], one_dev(one.fwd))

    for name in "ab":
        first_forward(name)

    for k in range(3):
        msgs.land(("v1", k))
    vec_sum[...] = vec_ref[...] + vec_one[0] + vec_one[1] + vec_one[2]
    for k, o in enumerate(z_others):
        msgs.send(("v2", k), vec_sum, vec_two.at[k], z_dev(o))

    for a, src, _ in arrays:
        msgs.land(("sib", a, "bwd"))
        msgs.land(("y", a, 0))
        gathered(a, src, "fwd", 2, extra=0)
        msgs.send(("y", a, 2), held.at[a, 2], from_y.at[a, 2], y_dev(ring_y.fwd))

    def first_total(name):
        one, _, two, two_dev, part, h = half(name)
        msgs.land((name, "one", 1))
        msgs.land((name, "one", 2))
        block_of = part(one.own)

        def add(r):
            v = block_of[:, r, :].astype(F32) + from_one[h, 1, :, r, :].astype(F32)
            held_two[h, :, r, :] = (v + from_one[h, 2, :, r, :].astype(F32)).astype(BF)

        slabs(48, 16, add)
        msgs.send((name, "two", 0), held_two.at[h, two.opp], from_two.at[h, 0], two_dev(two.fwd))
        msgs.send((name, "two", 1), held_two.at[h, two.bwd], from_two.at[h, 1], two_dev(two.bwd))

    for name in "ab":
        first_total(name)

    for k in range(3):
        msgs.land(("v2", k))
    vec_all[t] = vec_sum[...] + vec_two[0] + vec_two[1] + vec_two[2]
    for k, o in enumerate(others):
        msgs.send(("v3", k), vec_all.at[t], vec_all.at[t], group_member(x, z, o))

    for name in "ab":
        _, _, two, two_dev, _, h = half(name)
        msgs.land((name, "two", 0))
        held_last[h] = (held_two[h, two.fwd].astype(F32) + from_two[h, 0].astype(F32)).astype(BF)
        msgs.send((name, "two", 2), held_last.at[h], from_two.at[h, 2], two_dev(two.fwd))

    for a, src, dst in arrays:
        msgs.land(("sib", a, "own"))
        msgs.land(("y", a, 1))
        msgs.land(("y", a, 2))

        def add(r, a=a, src=src, dst=dst):
            v = src[mine(y), r, :].astype(F32) + sib[a, y, r, :].astype(F32)
            dst[r, :] = v + from_y[a, 1, r, :].astype(F32) + from_y[a, 2, r, :].astype(F32)

        slabs(256, 32, add)

    for name in "ab":
        _, _, two, _, _, h = half(name)
        msgs.land((name, "two", 1))
        msgs.land((name, "two", 2))
        v = held_two[h, two.own].astype(F32) + from_two[h, 1].astype(F32) + from_two[h, 2].astype(F32)
        own_ref[h * 6 : h * 6 + 6] = v.reshape(6, 8, 1024)
    for k, o in enumerate(others):
        msgs.send(("n", k), own_ref.at[o], all_ref.at[t], group_member(x, z, o))
    all_ref[t] = own_ref[t]
    msgs.finish()


def add_up(out_part, g_part, blob, vec):
    vmem = pl.BlockSpec(memory_space=pltpu.VMEM)
    return pl.pallas_call(
        sum_kernel,
        out_shape=(
            jax.ShapeDtypeStruct((256, 1024), F32),
            jax.ShapeDtypeStruct((256, 1024), F32),
            jax.ShapeDtypeStruct((8, 8, 1024), F32),
            jax.ShapeDtypeStruct((12, 8, 1024), F32),
            jax.ShapeDtypeStruct((8, 8, 256), F32),
        ),
        in_specs=[vmem] * 4,
        out_specs=(vmem,) * 5,
        scratch_shapes=[
            pltpu.VMEM((2, 4, 256, 1024), BF),
            pltpu.VMEM((2, 3, 256, 1024), BF),
            pltpu.VMEM((2, 3, 256, 1024), BF),
            pltpu.VMEM((2, 3, 4, 48, 1024), BF),
            pltpu.VMEM((2, 4, 48, 1024), BF),
            pltpu.VMEM((2, 3, 48, 1024), BF),
            pltpu.VMEM((2, 4, 48, 1024), BF),
            pltpu.VMEM((2, 48, 1024), BF),
            pltpu.VMEM((3, 8, 256), F32),
            pltpu.VMEM((8, 256), F32),
            pltpu.VMEM((3, 8, 256), F32),
            pltpu.SemaphoreType.DMA((SUM_MESSAGES,)),
            pltpu.SemaphoreType.DMA((SUM_MESSAGES,)),
        ],
        compiler_params=pltpu.CompilerParams(
            collective_id=1, has_side_effects=True, vmem_limit_bytes=VMEM_LIMIT
        ),
        name="sum_rows_and_gradients",
    )(out_part, g_part, blob, vec)


def body(tokens, segments, grad_out, ln1_gain, ln1_bias, ln2_gain, ln2_bias, w_qkv, b_qkv,
         w_dense, b_dense, w_fc1, b_fc1, w_fc2, b_fc2):
    me = lax.axis_index("fsdp")
    t = lax.rem(me, 8)

    dense = lax.ppermute(w_dense, "fsdp", [(d, (d % 16) * 8 + d // 16) for d in range(128)])
    small = jnp.concatenate(
        [ln1_gain, ln1_bias, ln2_gain, ln2_bias, b_qkv, b_fc1, b_dense, b_fc2, jnp.zeros((24,), BF)]
    )
    qkv_parts = w_qkv.reshape(8, 3, 8, 128).transpose(2, 0, 1, 3).reshape(8, 8, 384)
    fc1_parts = w_fc1.reshape(8, 16, 8, 32).transpose(2, 0, 1, 3).reshape(8, 8, 512)
    wl = jnp.concatenate([qkv_parts, fc1_parts, jnp.broadcast_to(small, (8, 8, 128))], -1)
    rest = jnp.concatenate([dense[None], w_fc2.reshape(4, 8, 1024)], 0)
    x_all, dy_all, seg_all, blob = gather(tokens, grad_out, segments, wl, rest)

    blob = blob.reshape(16, 13, 8, 1024)
    w1 = blob[:, 0:8].reshape(1024, 1024)
    w2 = jnp.concatenate([blob[:, 8].reshape(128, 1024), blob[:, 9:13].reshape(512, 1024)], 0)
    small = blob[:, 0:8, 0, 896:1000].reshape(128, 104)
    ln = small[:, 0:32].reshape(128, 4, 8).transpose(1, 0, 2).reshape(4, 1024).astype(F32)
    b_one = lax.dynamic_index_in_dim(small[:, 32:56].reshape(3, 8, 128), t, 1, False).reshape(384)
    b_two = lax.dynamic_index_in_dim(small[:, 56:88].reshape(16, 8, 32), t, 1, False).reshape(512)
    bias = jnp.concatenate([b_one, b_two])[None].astype(F32)
    b_out = (small[:, 88:96].astype(F32) + small[:, 96:104].astype(F32)).reshape(1024)

    out_part, g_part, grads, sums = block(x_all, dy_all, seg_all, w1, w2, ln, bias)
    out_sum, g_sum, n_all, own, sums = add_up(
        out_part, g_part, grads.reshape(4, 4, 96, 1024), sums[0:2].reshape(8, 256)
    )

    live = (segments.reshape(256, 1) >= 0).astype(F32)
    x = tokens.astype(F32)
    out = (x + live * (out_sum + b_out)).astype(BF)
    centre = x - jnp.mean(x, -1, keepdims=True)
    scale = lax.rsqrt(jnp.mean(centre * centre, -1, keepdims=True) + NORM_EPS)
    normed = centre * scale
    dx = (g_sum - jnp.mean(g_sum, -1, keepdims=True) - normed * jnp.mean(g_sum * normed, -1, keepdims=True)) * scale
    grad_tokens = (grad_out.astype(F32) + dx).astype(BF)

    sums = sums.reshape(8, 2, 1024)
    sum_qkv = sums[:, 0, 0:384].reshape(8, 3, 128).transpose(1, 0, 2).reshape(3072)
    sum_fc1 = sums[:, 0, 384:896].reshape(8, 16, 32).transpose(1, 0, 2).reshape(4096)
    n_qkv = n_all[:, :, 0:384].reshape(8, 8, 3, 128).transpose(1, 2, 0, 3).reshape(8, 3072)
    n_fc1 = n_all[:, :, 384:896].reshape(8, 8, 16, 32).transpose(1, 2, 0, 3).reshape(8, 4096)

    def norm_grads(weight, n, s, gain, bias_of):
        weight = weight.astype(F32)
        grad_w = gain.astype(F32)[:, None] * n + bias_of.astype(F32)[:, None] * s
        return jnp.sum(weight * n, 1), jnp.sum(weight * s, 1), grad_w

    g1_gain, g1_bias, grad_qkv = norm_grads(w_qkv, n_qkv, sum_qkv, ln1_gain, ln1_bias)
    g2_gain, g2_bias, grad_fc1 = norm_grads(w_fc1, n_fc1, sum_fc1, ln2_gain, ln2_bias)
    grad_b_qkv = lax.dynamic_slice(sum_qkv, (me * 24,), (24,))
    grad_b_fc1 = lax.dynamic_slice(sum_fc1, (me * 32,), (32,))
    grad_b_out = lax.dynamic_slice(sums[0, 1], (me * 8,), (8,))
    grad_dense = lax.ppermute(own[0:8, :, 896:1024], "fsdp", [(d, (d % 8) * 16 + d // 8) for d in range(128)])
    grad_dense = grad_dense.transpose(1, 0, 2).reshape(8, 1024)
    grad_fc2 = own[8:12].reshape(32, 1024)
    return (out, grad_tokens, g1_gain, g1_bias, g2_gain, g2_bias, grad_qkv, grad_b_qkv,
            grad_dense, grad_b_out, grad_fc1, grad_b_fc1, grad_fc2, grad_b_out)


def solution(mesh):
    rows, flat = P("fsdp", None), P("fsdp")
    return jax.shard_map(
        body,
        mesh=mesh,
        in_specs=(rows, rows, rows, flat, flat, flat, flat, rows, flat, rows, flat, rows, flat, rows, flat),
        out_specs=(rows, rows, flat, flat, flat, flat, rows, flat, rows, flat, rows, flat, rows, flat),
        check_vma=False,
    )
```

time: 2500 us -> 216 us (0.09)
  waiting for transfers between devices: 2170 us -> 0.01 us
  Pallas kernels: 0 us -> 169 us
  blocking collectives: 135 us -> 0 us
  matrix products: 121 us -> 0 us
    reduce_scatter x4 -> x0, waiting for transfers between devices: 2030 us -> none  [the longest x1 662 us: body(): lax.psum_scatter(totals[10], 'fsdp', scatter_dimension=0, tiled=True)]
    pallas_call x0 -> x3, Pallas kernels: none -> 169 us  [the longest x1 74.5 us: gather(): pl.pallas_call(gather_kernel, out_shape=(jax.ShapeDtypeStruct((8, 256, 10...]
    all_gather x4 -> x0, waiting for transfers between devices: 140 us -> none  [the longest x1 60.8 us: body(): lax.all_gather(w_fc2, 'fsdp', axis=0, tiled=True)]
    unnamed x2 -> x0, blocking collectives: 135 us -> none
    dot_general x34 -> x0, matrix products: 117 us -> none  [the longest x8 37.8 us: dot_float(): return jnp.dot(left, right, preferred_element_type=jnp.float32)]
  transfers between devices with their start and end apart: 8 -> 2, of which waited for: 7 -> 0; matrix products, arithmetic and copies ran while one was open for 6% -> 8% of each run, Pallas kernels for 0% -> 0%
where the time goes in v1:
time: 216 us; the launch traced here: 215 us
  Pallas kernels  169 us (78%)
  local copies, waits for them, and re-layouts  25.5 us (12%)
  other arithmetic  11 us (5%)
  starting transfers between devices  8.6 us (4%)
    pallas_call x1, Pallas kernels, gather(): pl.pallas_call(gather_kernel, out_shape=(jax.ShapeDtypeStruct((8, 256, 10...  74.5 us
    pallas_call x1, Pallas kernels, add_up(): pl.pallas_call(sum_kernel, out_shape=(jax.ShapeDtypeStruct((256, 1024), F...  52.2 us
    pallas_call x1, Pallas kernels, block(): pl.pallas_call(block_kernel, grid=(8,), out_shape=(jax.ShapeDtypeStruct((...  42 us
    concatenate x1, local copies, waits for them, and re-layouts, body(): jnp.concatenate([ln1_gain, ln1_bias, ln2_gain, ln2_bias, b_qkv, b_fc1, b_...  5.44 us
    ppermute x1, starting transfers between devices, body(): lax.ppermute(w_dense, 'fsdp', [(d, d % 16 * 8 + d // 16) for d in range(1...  5.07 us
  transfers between devices with their start and end apart: 2, of which 0 were waited for; matrix products, arithmetic and copies ran while one was open for 8% of the time, Pallas kernels for 0%

profile of v1, /device:TPU:1, one launch (start us, length us, event | category | flops | bytes accessed | tf_op | source)
XLA Modules:
  0.0 214.8 jit_solution(18356741803369803537)
XLA Ops:
  0.7 5.1 %collective-permute-start = (bf16[8,1024]{1,0:T(8,128)(2,1)}, bf16[8,1024]{1,0:T(8,128)(2,1)S(1)}, u32[]{:S(2)}, u32[]{:S(2)}) collective-permute-start(bf16[8,1024]{1,0:T(8,128)(2,1)} %param.25), channel_id=1, source_target_pairs={{0,0},{1,8},{2,16},{3,24},{4,32},{5,40},{6,48},{7,56},{8,64},{9,72... | collective-permute-start | bytes 49160 | tf_op jit(solution)/shard_map/ppermute | solution.py:591
  5.8 0.7 fusion.15
  6.5 1.2 convert_reduce_fusion
  7.7 1.3 fusion.9
  9.0 0.8 copy.71
  9.8 1.1 reshape.173
  10.9 0.2 reshape.174
  11.2 5.4 %concatenate.26 = bf16[128]{0:T(256)(128)(2,1)S(1)} concatenate(bf16[8]{0:T(256)(128)(2,1)} %param.19, bf16[8]{0:T(256)(128)(2,1)} %param.20, bf16[8]{0:T(256)(128)(2,1)} %param.21, bf16[8]{0:T(256)(128)(2,1)} %param.22, bf16[24]{0:T(256)(128)(2,1)} %param.24, bf16[32]{0:T(256)(128)(2,1)} %param.28, bf16[8]{0:T(256)(128)(2,1)} %param.26, bf16[8]{0:T(256)(128)(2,1)} %param.30, ...), dimensions={0} | concatenate | bytes 512 | tf_op jit(solution)/shard_map/concatenate | solution.py:592
  16.6 0.7 maximum_maximum_fusion.wl_ref
  17.4 0.6 pad_maximum_fusion.1.rest_ref
  18.0 74.5 %gather_rows_and_weights.1 = (bf16[8,256,1024]{2,1,0:T(8,128)(2,1)}, bf16[8,256,1024]{2,1,0:T(8,128)(2,1)}, s32[8,2,128]{2,1,0:T(2,128)}, bf16[4,4,13,8,1024]{4,3,2,1,0:T(8,128)(2,1)}) custom-call(bf16[256,1024]{1,0:T(8,128)(2,1)} %x_ref.1, bf16[256,1024]{1,0:T(8,128)(2,1)} %dy_ref.1, s32[2,128]{1,0:T(2,128)} %seg_ref.1, ...), custom_call_target="tpu_custom_call" | custom-call | tf_op jit(solution)/shard_map/gather_rows_and_weights/pallas_call | solution.py:209
  92.6 1.0 slice.71
  93.6 0.1 slice.73
  93.7 0.1 convert_add_fusion.1
  93.8 0.1 slice_bitcast_fusion.3
  93.9 1.0 slice_bitcast_fusion
  94.8 1.3 slice.70
  96.2 3.2 %slice.68 = bf16[16,8,8,1024]{3,2,1,0:T(8,128)(2,1)} slice(bf16[16,13,8,1024]{3,2,1,0:T(8,128)(2,1)} %bitcast.62), slice={[0:16], [0:8], [0:8], [0:1024]} | slice | bytes 4194304 | tf_op jit(solution)/shard_map/slice | solution.py:602
  99.4 0.1 reshape.179
  99.5 0.1 concatenate.31
  99.7 0.2 copy.56
  99.9 0.8 reshape.191.ln_ref
  100.6 0.6 maximum_convert_fusion.bias_ref
  101.2 1.2 pad_maximum_fusion.w2_ref
  102.4 42.0 %block_forward_backward.1 = (bf16[8,256,1024]{2,1,0:T(8,128)(2,1)}, bf16[8,256,1024]{2,1,0:T(8,128)(2,1)}, bf16[16,96,1024]{2,1,0:T(8,128)(2,1)}, f32[8,1024]{1,0:T(8,128)}) custom-call(bf16[8,256,1024]{2,1,0:T(8,128)(2,1)} %get-tuple-element.27.x_ref, bf16[8,256,1024]{2,1,0:T(8,128)(2,1)} %get-tuple-element.28.dy_ref, ...), custom_call_target="tpu_custom_call" | custom-call | flops 20000000000 | bytes 25000000 | tf_op jit(solution)/shard_map/block_forward_backward/pallas_call | solution.py:368
  144.4 0.8 slice.58
  145.1 0.6 reshape.182.vec_ref
  145.7 52.2 %sum_rows_and_gradients.1 = (f32[256,1024]{1,0:T(8,128)}, f32[256,1024]{1,0:T(8,128)}, f32[8,8,1024]{2,1,0:T(8,128)}, f32[12,8,1024]{2,1,0:T(8,128)}, f32[8,8,256]{2,1,0:T(8,128)}) custom-call(bf16[8,256,1024]{2,1,0:T(8,128)(2,1)} %get-tuple-element.31.out_ref, bf16[8,256,1024]{2,1,0:T(8,128)(2,1)} %get-tuple-element.32.g_ref, ...), custom_call_target="tpu_custom_call" | custom-call | tf_op jit(solution)/shard_map/sum_rows_and_gradients/pallas_call | solution.py:553
  197.9 0.9 slice.65
  198.8 1.6 slice_bitcast_fusion.1
  200.4 0.9 reshape.185
  201.4 0.9 slice_bitcast_fusion.2
  202.3 0.9 slice.63
  203.2 0.1 add.53
  203.3 3.5 %collective-permute-start.1 = (f32[8,8,128]{2,1,0:T(8,128)S(1)}, f32[8,8,128]{2,1,0:T(8,128)S(1)}, u32[]{:S(2)}, u32[]{:S(2)}) collective-permute-start(f32[8,8,128]{2,1,0:T(8,128)S(1)} %slice.65), channel_id=1, source_target_pairs={{0,0},{1,16},{2,32},{3,48},{4,64},{5,80},{6,96},{7,112},{8,1},{9,1... | collective-permute-start | bytes 98312 | tf_op jit(solution)/shard_map/ppermute | solution.py:641
  206.9 0.1 reshape_squeeze.15
  207.0 0.1 mul.123
  207.1 0.2 reshape.186
  207.2 0.3 copy.59
  207.6 0.2 reshape.187
  207.8 0.3 fusion.17
  208.2 1.4 fusion.14
  209.6 1.4 fusion.12
  211.0 1.5 fusion.8
  212.5 0.6 dynamic_slice.21
  213.1 0.6 dynamic_slice.24
  213.7 0.5 copy.76
  214.2 0.6 copy.77
  (48 shorter events, 0.5 us)
Async XLA Ops:
  0.6 16.7 %copy-start.10 = (bf16[8]{0:T(256)(128)(2,1)S(1)}, bf16[8]{0:T(256)(128)(2,1)}, u32[]{:S(2)}) copy-start(bf16[8]{0:T(256)(128)(2,1)} %param.22) | copy-start | bytes 52
  0.7 16.7 %copy-start.9 = (bf16[8]{0:T(256)(128)(2,1)S(1)}, bf16[8]{0:T(256)(128)(2,1)}, u32[]{:S(2)}) copy-start(bf16[8]{0:T(256)(128)(2,1)} %param.21) | copy-start | bytes 52
  0.7 16.6 %copy-start.8 = (bf16[8]{0:T(256)(128)(2,1)S(1)}, bf16[8]{0:T(256)(128)(2,1)}, u32[]{:S(2)}) copy-start(bf16[8]{0:T(256)(128)(2,1)} %param.20) | copy-start | bytes 52
  0.7 16.6 %copy-start.7 = (bf16[8]{0:T(256)(128)(2,1)S(1)}, bf16[8]{0:T(256)(128)(2,1)}, u32[]{:S(2)}) copy-start(bf16[8]{0:T(256)(128)(2,1)} %param.19) | copy-start | bytes 52
  0.7 16.7 %copy-start.6 = (bf16[32,1024]{1,0:T(8,128)(2,1)S(1)}, bf16[32,1024]{1,0:T(8,128)(2,1)}, u32[]{:S(2)}) copy-start(bf16[32,1024]{1,0:T(8,128)(2,1)} %param.29) | copy-start | bytes 196612
  0.7 16.7 %collective-permute-start = (bf16[8,1024]{1,0:T(8,128)(2,1)}, bf16[8,1024]{1,0:T(8,128)(2,1)S(1)}, u32[]{:S(2)}, u32[]{:S(2)}) collective-permute-start(bf16[8,1024]{1,0:T(8,128)(2,1)} %param.25), channel_id=1, source_target_pairs={{0,0},{1,8},{2,16},{3,24},{4,32},{5,40},{6,48},{7,56},{8,64},{9,72... | collective-permute-start | bytes 49160 | tf_op jit(solution)/shard_map/ppermute | solution.py:591
  197.9 9.9 %copy-start = (bf16[256,1024]{1,0:T(8,128)(2,1)S(1)}, bf16[256,1024]{1,0:T(8,128)(2,1)}, u32[]{:S(2)}) copy-start(bf16[256,1024]{1,0:T(8,128)(2,1)} %x_ref.1) | copy-start | bytes 1572868
  197.9 9.9 %copy-start.1 = (f32[256,1024]{1,0:T(8,128)S(1)}, f32[256,1024]{1,0:T(8,128)}, u32[]{:S(2)}) copy-start(f32[256,1024]{1,0:T(8,128)} %get-tuple-element.36) | copy-start | bytes 3145732
  200.4 7.8 %copy-start.5 = (bf16[8,3072]{1,0:T(8,128)(2,1)S(1)}, bf16[8,3072]{1,0:T(8,128)(2,1)}, u32[]{:S(2)}) copy-start(bf16[8,3072]{1,0:T(8,128)(2,1)} %param.23) | copy-start | bytes 147460
  201.3 8.2 %copy-start.4 = (bf16[8,4096]{1,0:T(8,128)(2,1)S(1)}, bf16[8,4096]{1,0:T(8,128)(2,1)}, u32[]{:S(2)}) copy-start(bf16[8,4096]{1,0:T(8,128)(2,1)} %param.27) | copy-start | bytes 196612
  203.2 7.8 %copy-start.2 = (bf16[256,1024]{1,0:T(8,128)(2,1)S(1)}, bf16[256,1024]{1,0:T(8,128)(2,1)}, u32[]{:S(2)}) copy-start(bf16[256,1024]{1,0:T(8,128)(2,1)} %dy_ref.1) | copy-start | bytes 1572868
  203.3 10.4 %collective-permute-start.1 = (f32[8,8,128]{2,1,0:T(8,128)S(1)}, f32[8,8,128]{2,1,0:T(8,128)S(1)}, u32[]{:S(2)}, u32[]{:S(2)}) collective-permute-start(f32[8,8,128]{2,1,0:T(8,128)S(1)} %slice.65), channel_id=1, source_target_pairs={{0,0},{1,16},{2,32},{3,48},{4,64},{5,80},{6,96},{7,112},{8,1},{9,1... | collective-permute-start | bytes 98312 | tf_op jit(solution)/shard_map/ppermute | solution.py:641
  207.8 3.2 %copy-start.3 = (f32[256,1024]{1,0:T(8,128)S(1)}, f32[256,1024]{1,0:T(8,128)}, u32[]{:S(2)}) copy-start(f32[256,1024]{1,0:T(8,128)} %get-tuple-element.35) | copy-start | bytes 3145732
  212.5 2.3 %copy-start.11 = (f32[8]{0:T(128)}, f32[8]{0:T(128)S(1)}, u32[]{:S(2)}) copy-start(f32[8]{0:T(128)S(1)} %fusion.16) | copy-start | bytes 100

commit v2 on v1

v2 whole, which is shorter than its diff:
```python
import functools
import math

import jax
import jax.numpy as jnp
import numpy as np
from jax import lax
from jax.experimental import pallas as pl
from jax.experimental.pallas import tpu as pltpu
from jax.sharding import PartitionSpec as P

NORM_EPS = 1e-05
MASKED = -1e30
MESH = pl.DeviceIdType.MESH
BF = jnp.bfloat16
F32 = jnp.float32
VMEM_LIMIT = 60 * 1024 * 1024


def coords():
    i = lax.axis_index("fsdp")
    core = lax.rem(i, 2)
    y = lax.rem(i // 2, 4)
    z = lax.rem(i // 8, 4)
    x = i // 32
    return x, z, y, core


def ident(x, z, y, core):
    return ((x * 4 + z) * 4 + y) * 2 + core


class Ring:
    def __init__(self, at, core):
        step = 1 + 2 * core
        self.own = at
        self.fwd = lax.rem(at + step, 4)
        self.bwd = lax.rem(at + 4 - step, 4)
        self.opp = lax.rem(at + 2, 4)


class Messages:
    def __init__(self, send_sem, recv_sem):
        self.send_sem, self.recv_sem = send_sem, recv_sem
        self.sent, self.landed = {}, set()

    def plan(self, name, src, dst, target):
        n = len(self.sent)
        copy = pltpu.make_async_remote_copy(
            src_ref=src,
            dst_ref=dst,
            send_sem=self.send_sem.at[n],
            recv_sem=self.recv_sem.at[n],
            device_id=(target,),
            device_id_type=MESH,
        )
        self.sent[name] = copy

    def send(self, name, src, dst, target):
        self.plan(name, src, dst, target)
        self.sent[name].start()

    def land(self, name):
        assert name not in self.landed
        self.landed.add(name)
        self.sent[name].wait_recv()

    def finish(self):
        for name, copy in self.sent.items():
            if name not in self.landed:
                copy.wait_recv()
        for copy in self.sent.values():
            copy.wait_send()


def enter(targets):
    barrier = pltpu.get_barrier_semaphore()
    for target in targets:
        pl.semaphore_signal(barrier, inc=1, device_id=(target,), device_id_type=MESH)
    pl.semaphore_wait(barrier, len(targets))


def group_member(x, z, t):
    return ident(x, z, 0, 0) + t


def dot(a, b):
    return jnp.dot(a, b, preferred_element_type=F32)


def dot_nt(a, b):
    return lax.dot_general(a, b, (((1,), (1,)), ((), ())), preferred_element_type=F32)


def dot_tn(a, b):
    return lax.dot_general(a, b, (((0,), (0,)), ((), ())), preferred_element_type=F32)


def turn(u, cosine, sine, low_lanes):
    moved = jnp.where(low_lanes, pltpu.roll(u, 120, 1), pltpu.roll(u, 8, 1))
    return u * cosine + moved * sine


def rotary_table():
    m = 8
    angle = np.arange(128, dtype=np.float64)[:, None] * (10000.0 ** (-2.0 * np.arange(m) / 16.0))[None, :]
    cosine = np.ones((128, 128), np.float32)
    sine = np.zeros((128, 128), np.float32)
    for head in (0, 64):
        cosine[:, head : head + m] = np.cos(angle)
        cosine[:, head + m : head + 2 * m] = np.cos(angle)
        sine[:, head : head + m] = -np.sin(angle)
        sine[:, head + m : head + 2 * m] = np.sin(angle)
    parts = []
    for table in (cosine, sine):
        high = table.astype(jnp.bfloat16)
        parts += [high, (table - high.astype(np.float32)).astype(jnp.bfloat16)]
    return np.concatenate(parts, 1)


def slabs(rows, step, fn):
    def one(i, carry):
        fn(pl.ds(pl.multiple_of(i * step, step), step))
        return carry

    lax.fori_loop(0, rows // step, one, 0)


class Half:
    def __init__(self, name, one, one_dev, two, two_dev, rows):
        self.name, self.one, self.one_dev, self.two, self.two_dev, self.rows = name, one, one_dev, two, two_dev, rows


def unpack_small(packed, t):
    packed = packed.astype(BF)

    def pick(lanes, columns, owner):
        j = lax.broadcasted_iota(jnp.int32, (128, lanes), 0)
        at = lax.broadcasted_iota(jnp.int32, (128, lanes), 1)
        of_row = ((j >> 3) & 3) * 32 + (j >> 5) * 8 + (j & 7)
        select = jnp.zeros((128, lanes), F32)
        for column in columns(at):
            select = select + (j == column).astype(F32)
        rows = dot(packed, select.astype(BF))
        return jnp.sum(jnp.where(of_row == owner(at), rows, 0.0), 0, keepdims=True)

    eight = lambda *starts: pick(1024, lambda at: [s + (at & 7) for s in starts], lambda at: at >> 3)
    ln = [eight(8 * v) for v in range(4)]
    b_out = eight(88, 96)
    qkv_at = lambda at: (at >> 7) * 1024 + t * 128 + (at & 127)
    d24 = lambda c: (c * 2731) >> 16
    b_qkv = pick(384, lambda at: [32 + qkv_at(at) - 24 * d24(qkv_at(at))], lambda at: d24(qkv_at(at)))
    b_fc1 = pick(512, lambda at: [56 + (at & 31)], lambda at: t * 16 + (at >> 5))
    return ln, b_qkv, b_fc1, b_out


def rows_pass(x, dy, seg, w1_ref, w2_ref, ln_ref, bias_ref, table_ref):
    x = x.astype(F32)
    centre = x - jnp.mean(x, 1, keepdims=True)
    spread = jnp.mean(centre * centre, 1, keepdims=True)
    normed = centre * lax.rsqrt(spread + NORM_EPS)
    g1, g2 = ln_ref[0:1, :], ln_ref[2:3, :]
    a1 = (normed * g1 + ln_ref[1:2, :]).astype(BF)
    a2 = (normed * g2 + ln_ref[3:4, :]).astype(BF)
    joined = dot(a1, w1_ref[:, 0:384]) + bias_ref[0:1, 0:384]
    hidden = dot(a2, w1_ref[:, 384:896]) + bias_ref[0:1, 384:896]
    phi_cdf = 0.5 + 0.5 * lax.erf(hidden * math.sqrt(0.5))
    active = hidden * phi_cdf
    slope = phi_cdf + hidden * (jnp.exp(hidden * hidden * -0.5) * (1.0 / math.sqrt(2.0 * math.pi)))

    row = lax.broadcasted_iota(jnp.int32, (128, 128), 0)
    col = lax.broadcasted_iota(jnp.int32, (128, 128), 1)
    masks, lives, tables = [], [], []
    for b in range(2):
        seg_c = jnp.broadcast_to(seg[b : b + 1, :].astype(F32), (128, 128))
        seg_r = seg_c.T
        allowed = (seg_c == seg_r) & (col <= row)
        position = jnp.sum(allowed.astype(F32), 1, keepdims=True) - 1.0
        onehot = (col == position.astype(jnp.int32)).astype(BF)
        tables.append(dot(onehot, table_ref[...]))
        masks.append(allowed)
        lives.append((seg_r[:, 0:1] >= 0.0).astype(F32))
    live = jnp.concatenate(lives, 0)
    d_cat = dot_nt(dy, w2_ref[...]) * live
    d_hidden = d_cat[:, 128:640] * slope
    d_context = d_cat[:, 0:128].astype(BF)
    active = (active.astype(BF).astype(F32) * live).astype(BF)

    lane = lax.broadcasted_iota(jnp.int32, (128, 128), 1)
    low_lanes = (lane & 63) < 8
    head0 = lane < 64

    def stacked(u):
        zero = jnp.zeros_like(u)
        return jnp.concatenate([jnp.where(head0, u, zero), jnp.where(head0, zero, u)], 0)

    contexts, d_joined = [], []
    for b in range(2):
        part = slice(b * 128, b * 128 + 128)
        cosine = tables[b][:, 0:128] + tables[b][:, 128:256]
        sine = tables[b][:, 256:384] + tables[b][:, 384:512]
        q = turn(joined[part, 0:128], cosine, sine, low_lanes).astype(BF)
        k = turn(joined[part, 128:256], cosine, sine, low_lanes).astype(BF)
        v = joined[part, 256:384].astype(BF)
        q2 = stacked(q)
        allowed = jnp.concatenate([masks[b], masks[b]], 0)
        scores = jnp.where(allowed, dot_nt(q2, k) * 0.125, MASKED)
        e = jnp.exp(scores - jnp.max(scores, 1, keepdims=True))
        probs = e / jnp.sum(e, 1, keepdims=True)
        probs_b = probs.astype(BF)
        ctx = dot(probs_b, v)
        ctx = jnp.where(head0, ctx[0:128], ctx[128:256]).astype(BF).astype(F32)
        contexts.append((ctx * lives[b]).astype(BF))
        dc2 = stacked(d_context[part])
        d_probs = dot_nt(dc2, v)
        d_v = dot_tn(probs_b, dc2)
        d_scores = probs * (d_probs - jnp.sum(probs * d_probs, 1, keepdims=True))
        d_scores = d_scores.astype(BF)
        dq2 = dot(d_scores, k) * 0.125
        d_q = jnp.where(head0, dq2[0:128], dq2[128:256])
        d_k = dot_tn(d_scores, q2) * 0.125
        d_joined.append(
            jnp.concatenate(
                [turn(d_q, cosine, -sine, low_lanes), turn(d_k, cosine, -sine, low_lanes), d_v], 1
            )
        )
    cat = jnp.concatenate([jnp.concatenate(contexts, 0), active], 1)
    out = dot(cat, w2_ref[...])
    d_all = jnp.concatenate([jnp.concatenate(d_joined, 0), d_hidden], 1)
    column_sums = jnp.sum(d_all, 0, keepdims=True), jnp.sum(dy.astype(F32) * live, 0, keepdims=True)
    d_all_b = d_all.astype(BF)
    g = g1 * dot_nt(d_all_b[:, 0:384], w1_ref[:, 0:384]) + g2 * dot_nt(d_all_b[:, 384:896], w1_ref[:, 384:896])
    return out, g, normed.astype(BF), d_all_b, cat, column_sums


SCRATCH = dict(
    X=((8, 256, 1024), BF),
    DY=((8, 256, 1024), BF),
    SEG=((8, 2, 128), jnp.int32),
    SM=((8, 8, 128), F32),
    AW=((8, 8, 896), BF),
    WA=((4, 4, 64, 896), BF),
    WB=((4, 4, 48, 1024), BF),
    w1=((1024, 896), BF),
    w2=((640, 1024), BF),
    ln=((8, 1024), F32),
    bias=((8, 896), F32),
    OUT=((8, 256, 1024), BF),
    G=((8, 256, 1024), BF),
    NB=((8, 256, 1024), BF),
    DALL=((8, 256, 896), BF),
    CAT=((8, 256, 640), BF),
    sums=((8, 1024), F32),
    sib=((2, 4, 256, 1024), BF),
    from_y=((2, 3, 256, 1024), BF),
    ga=((4, 4, 64, 896), BF),
    gb=((4, 4, 48, 1024), BF),
    one_a=((3, 4, 64, 896), BF),
    one_b=((3, 4, 48, 1024), BF),
    held_one_a=((4, 64, 896), BF),
    held_one_b=((4, 48, 1024), BF),
    two_a=((3, 64, 896), BF),
    two_b=((3, 48, 1024), BF),
    held_two_a=((4, 64, 896), BF),
    held_two_b=((4, 48, 1024), BF),
    last_a=((64, 896), BF),
    last_b=((48, 1024), BF),
    fin_a=((8, 8, 896), F32),
    vec=((8, 256), F32),
    vec_one=((3, 8, 256), F32),
    vec_sum=((8, 256), F32),
    vec_two=((3, 8, 256), F32),
)
MESSAGES = 7 * 6 + 2 * 7 + 2 * (3 + 12) + 13 + 2 * (4 + 3) + 2 * 6 + 7


def whole_kernel(x_ref, dy_ref, seg_ref, wqkv_ref, wfc1_ref, dense_ref, fc2_ref, small_ref, table_ref,
                 out_sum, g_sum, n_all, own_b, vec_all, b_out, *scratch):
    m = dict(zip(SCRATCH, scratch))
    send_sem, recv_sem = scratch[len(SCRATCH) :]
    X, DY, SEG, SM, AW, WA, WB = (m[k] for k in ("X", "DY", "SEG", "SM", "AW", "WA", "WB"))
    x, z, y, core = coords()
    t = y * 2 + core
    ring_y, ring_x, ring_z = Ring(y, core), Ring(x, core), Ring(z, core)
    y_dev = lambda to: ident(x, z, to, core)
    x_dev = lambda to: ident(to, z, y, core)
    z_dev = lambda to: ident(x, to, y, core)
    sibling = ident(x, z, y, 1 - core)
    others = [lax.rem(t + k, 8) for k in range(1, 8)]
    x_others = [lax.rem(x + k, 4) for k in range(1, 4)]
    z_others = [lax.rem(z + k, 4) for k in range(1, 4)]
    mine = lambda at: at * 2 + core
    hers = lambda at: at * 2 + 1 - core
    halves = (
        Half("a", ring_x, x_dev, ring_z, z_dev, 64),
        Half("b", ring_z, z_dev, ring_x, x_dev, 48),
    )
    enter([group_member(x, z, o) for o in others] + [x_dev(o) for o in x_others] + [z_dev(o) for o in z_others])
    msgs = Messages(send_sem, recv_sem)

    for k, o in enumerate(others):
        dev = group_member(x, z, o)
        for sec in range(3):
            lanes = pl.ds(pl.multiple_of(sec * 1024 + o * 128, 128), 128)
            msgs.send(("w", k, sec), wqkv_ref.at[:, lanes], AW.at[t, :, pl.ds(sec * 128, 128)], dev)
        lanes = pl.ds(pl.multiple_of(o * 512, 512), 512)
        msgs.send(("w", k, 3), wfc1_ref.at[:, lanes], AW.at[t, :, pl.ds(384, 512)], dev)
        msgs.send(("w", k, 4), small_ref, SM.at[t], dev)
    rows = (("x", x_ref, X), ("d", dy_ref, DY))

    def own_rows(name, src, dst):
        msgs.send((name, 0), src, dst.at[t], y_dev(ring_y.fwd))
        msgs.send((name, 1), src, dst.at[t], y_dev(ring_y.bwd))
        msgs.send((name, 2), src, dst.at[t], sibling)

    own_rows(*rows[0])
    for k, o in enumerate(others):
        msgs.send(("s", k), seg_ref, SEG.at[t], group_member(x, z, o))
    own_rows(*rows[1])
    for sec in range(3):
        lanes = pl.ds(pl.multiple_of(sec * 1024 + t * 128, 128), 128)
        AW[t, :, sec * 128 : sec * 128 + 128] = wqkv_ref[:, lanes]
    AW[t, :, 384:896] = wfc1_ref[:, pl.ds(pl.multiple_of(t * 512, 512), 512)]
    SM[t] = small_ref[...]
    X[t] = x_ref[...]
    DY[t] = dy_ref[...]
    SEG[t] = seg_ref[...]
    for k in range(7):
        for sec in range(5):
            msgs.land(("w", k, sec))
    for pair in range(4):
        both = jnp.concatenate([AW[2 * pair].astype(F32), AW[2 * pair + 1].astype(F32)], 0)
        WA[x, z, 16 * pair : 16 * pair + 16, :] = both.astype(BF)
    member = lax.broadcasted_iota(jnp.int32, (8, 128), 0)
    small = jnp.zeros((8, 128), F32)
    for k in range(8):
        small = jnp.where(member == k, SM[k], small)
    small = jnp.concatenate([small, jnp.zeros((8, 896), F32)], 1)
    WB[z, x, 0:16, :] = jnp.concatenate([dense_ref[...].astype(F32), small], 0).astype(BF)
    WB[z, x, 16:48, :] = fc2_ref[...]

    gathered = {"a": WA, "b": WB}

    def first(h, k, at, to):
        ref = gathered[h.name].at[at, h.two.own]
        msgs.send((h.name, "p", k), ref, ref, h.one_dev(to))

    def second(h, sub, k, at, frm, to):
        ref = gathered[h.name].at[at, frm]
        msgs.send((h.name, sub, k), ref, ref, h.two_dev(to))

    def spread(h, sub):
        at = getattr(h.one, sub)
        second(h, sub, 0, at, h.two.own, h.two.fwd)
        second(h, sub, 1, at, h.two.own, h.two.bwd)

    def pass_on(h, sub):
        msgs.land((h.name, sub, 0))
        second(h, sub, 2, getattr(h.one, sub), h.two.bwd, h.two.fwd)

    for h in halves:
        first(h, 0, h.one.own, h.one.fwd)
        first(h, 1, h.one.own, h.one.bwd)
        spread(h, "own")
    for h in halves:
        msgs.land((h.name, "p", 0))
        first(h, 2, h.one.bwd, h.one.fwd)
        spread(h, "bwd")
    for h in halves:
        msgs.land((h.name, "p", 1))
        spread(h, "fwd")
    for h in halves:
        msgs.land((h.name, "p", 2))
        spread(h, "opp")
    for h in halves:
        pass_on(h, "own")

    def rows_on(name, dst):
        msgs.land((name, 0))
        ref = dst.at[mine(ring_y.bwd)]
        msgs.send((name, 3), ref, ref, y_dev(ring_y.fwd))
        msgs.send((name, 4), ref, ref, sibling)
        msgs.land((name, 1))
        ref = dst.at[mine(ring_y.fwd)]
        msgs.send((name, 5), ref, ref, sibling)

    def rows_last(name, dst):
        msgs.land((name, 3))
        ref = dst.at[mine(ring_y.opp)]
        msgs.send((name, 6), ref, ref, sibling)

    rows_on("x", X)
    for sub in ("bwd", "fwd", "opp"):
        for h in halves:
            pass_on(h, sub)
    rows_on("d", DY)
    rows_last("x", X)
    for k in range(7):
        msgs.land(("s", k))
    for h in halves:
        for sub in ("own", "bwd", "fwd", "opp"):
            msgs.land((h.name, sub, 1))
            msgs.land((h.name, sub, 2))

    w1, w2, ln, bias = m["w1"], m["w2"], m["ln"], m["bias"]
    w1[...] = WA[...].reshape(1024, 896)
    mixed = WB[:, :, 0:16, :].astype(F32)
    w2[0:128, :] = mixed[:, :, 0:8, :].reshape(128, 1024).astype(BF)
    w2[128:640, :] = WB[:, :, 16:48, :].reshape(512, 1024)
    norms, b_qkv, b_fc1, b_both = unpack_small(mixed[:, :, 8:16, 0:128].reshape(128, 128), t)
    for v in range(4):
        ln[v : v + 1, :] = norms[v]
    bias[0:1, 0:384] = b_qkv
    bias[0:1, 384:896] = b_fc1
    b_out[...] = jnp.broadcast_to(b_both, (8, 1024))
    sums = m["sums"]
    sums[...] = jnp.zeros_like(sums)

    OUT, G, NB, DALL, CAT, sib, from_y = (m[k] for k in ("OUT", "G", "NB", "DALL", "CAT", "sib", "from_y"))
    arrays = ((0, OUT, out_sum), (1, G, g_sum))
    chips = [lax.rem(y + k, 4) for k in (3, 1, 2, 0)]

    def join(a, src, at, extra=None):
        def add(r):
            v = src[mine(at), r, :].astype(F32) + sib[a, at, r, :].astype(F32)
            if extra is not None:
                v = v + from_y[a, extra, r, :].astype(F32)
            src[mine(at), r, :] = v.astype(BF)

        slabs(256, 32, add)

    ref = DY.at[mine(ring_y.opp)]
    msgs.plan(("d", 6), ref, ref, sibling)
    for a, src, _ in arrays:
        for k in range(4):
            msgs.plan(("sib", a, k), src.at[hers(chips[k])], sib.at[a, chips[k]], sibling)
        msgs.plan(("y", a, 1), src.at[mine(ring_y.bwd)], from_y.at[a, 1], y_dev(ring_y.bwd))
        msgs.plan(("y", a, 0), src.at[mine(ring_y.opp)], from_y.at[a, 0], y_dev(ring_y.fwd))

    def before(s):
        @pl.when(s == 0)
        def _():
            for name in "xd":
                msgs.land((name, 4))
                msgs.land((name, 5))

        @pl.when(s == 4)
        def _():
            msgs.land(("d", 3))
            msgs.sent["d", 6].start()
            msgs.land(("x", 6))
            msgs.land(("d", 6))

        @pl.when(s == 6)
        def _():
            msgs.land(("x", 2))
            msgs.land(("d", 2))

    def after(s):
        for k in range(4):

            @pl.when(s == 2 * k)
            def _(k=k):
                for a, src, _ in arrays:
                    msgs.sent["sib", a, k].start()

        @pl.when(s == 3)
        def _():
            for a, src, _ in arrays:
                msgs.land(("sib", a, 0))
                msgs.land(("sib", a, 1))
                join(a, src, ring_y.bwd)
                msgs.sent["y", a, 1].start()

        @pl.when(s == 5)
        def _():
            for a, src, _ in arrays:
                msgs.land(("sib", a, 2))
                join(a, src, ring_y.opp)
                msgs.sent["y", a, 0].start()

    def one_slot(s, carry):
        before(s)
        k = s // 2
        chip = jnp.where(k == 0, chips[0], jnp.where(k == 1, chips[1], jnp.where(k == 2, chips[2], chips[3])))
        slot = chip * 2 + jnp.where(s % 2 == 0, 1 - core, core)
        out, g, normed, d_all, cat, column_sums = rows_pass(
            X[slot], DY[slot], SEG[slot], w1, w2, ln, bias, table_ref
        )
        OUT[slot] = out.astype(BF)
        G[slot] = g.astype(BF)
        NB[slot] = normed
        DALL[slot] = d_all
        CAT[slot] = cat
        sums[0:1, 0:896] += column_sums[0]
        sums[1:2, :] += column_sums[1]
        after(s)
        return carry

    lax.fori_loop(0, 8, one_slot, 0)

    vec, vec_one, vec_sum, vec_two = (m[k] for k in ("vec", "vec_one", "vec_sum", "vec_two"))
    for i in range(8):
        vec[i : i + 1, :] = sums[i // 4 : i // 4 + 1, (i % 4) * 256 : (i % 4) * 256 + 256]
    for k, o in enumerate(x_others):
        msgs.send(("v1", k), vec, vec_one.at[k], x_dev(o))

    part = {"a": m["ga"], "b": m["gb"]}
    into_one = {"a": m["one_a"], "b": m["one_b"]}
    held_one = {"a": m["held_one_a"], "b": m["held_one_b"]}
    into_two = {"a": m["two_a"], "b": m["two_b"]}
    held_two = {"a": m["held_two_a"], "b": m["held_two_b"]}
    last = {"a": m["last_a"], "b": m["last_b"]}
    ha, hb = halves

    def grad_a(at):
        lanes = pl.ds(pl.multiple_of(at * 256, 256), 256)
        v = dot_tn(NB[:, :, lanes].reshape(2048, 256), DALL[...].reshape(2048, 896))
        part["a"][at] = v.reshape(4, 64, 896).astype(BF)

    def grad_b(first_at, second_at):
        cols = [
            CAT[:, :, pl.ds(pl.multiple_of(128 + at * 128, 128), 128)].reshape(2048, 128)
            for at in (first_at, second_at)
        ]
        v = dot_tn(jnp.concatenate(cols, 1), DY[...].reshape(2048, 1024))
        part["b"][first_at, :, 16:48, :] = v[0:128].reshape(4, 32, 1024).astype(BF)
        part["b"][second_at, :, 16:48, :] = v[128:256].reshape(4, 32, 1024).astype(BF)

    def send_one(h, k, at, to):
        msgs.send((h.name, "one", k), part[h.name].at[at], into_one[h.name].at[k], h.one_dev(to))

    v = dot_tn(CAT[:, :, 0:128].reshape(2048, 128), DY[...].reshape(2048, 1024)).reshape(4, 4, 8, 1024)
    part["b"][:, :, 0:16, :] = jnp.concatenate([v, jnp.zeros_like(v)], 2).astype(BF)
    grad_a(ring_x.opp)
    send_one(ha, 0, ring_x.opp, ring_x.fwd)
    grad_b(ring_z.opp, ring_z.bwd)
    send_one(hb, 0, ring_z.opp, ring_z.fwd)
    send_one(hb, 1, ring_z.bwd, ring_z.bwd)

    for a, src, _ in arrays:
        msgs.land(("y", a, 0))
        join(a, src, ring_y.fwd, extra=0)
        msgs.send(("y", a, 2), src.at[mine(ring_y.fwd)], from_y.at[a, 2], y_dev(ring_y.fwd))

    grad_a(ring_x.bwd)
    send_one(ha, 1, ring_x.bwd, ring_x.bwd)
    grad_a(ring_x.fwd)
    grad_b(ring_z.fwd, ring_z.own)

    for k in range(3):
        msgs.land(("v1", k))
    vec_sum[...] = vec[...] + vec_one[0] + vec_one[1] + vec_one[2]
    for k, o in enumerate(z_others):
        msgs.send(("v2", k), vec_sum, vec_two.at[k], z_dev(o))

    def slab_of(h):
        return h.rows // (4 if h.name == "a" else 3)

    def first_forward(h):
        msgs.land((h.name, "one", 0))

        def add(r):
            v = part[h.name][h.one.fwd, :, r, :].astype(F32) + into_one[h.name][0, :, r, :].astype(F32)
            held_one[h.name][:, r, :] = v.astype(BF)

        slabs(h.rows, slab_of(h), add)
        msgs.send((h.name, "one", 2), held_one[h.name], into_one[h.name].at[2], h.one_dev(h.one.fwd))

    for h in halves:
        first_forward(h)
    grad_a(ring_x.own)

    def first_total(h):
        msgs.land((h.name, "one", 1))
        msgs.land((h.name, "one", 2))

        def add(r):
            v = part[h.name][h.one.own, :, r, :].astype(F32) + into_one[h.name][1, :, r, :].astype(F32)
            held_two[h.name][:, r, :] = (v + into_one[h.name][2, :, r, :].astype(F32)).astype(BF)

        slabs(h.rows, slab_of(h), add)
        held = held_two[h.name]
        msgs.send((h.name, "two", 0), held.at[h.two.opp], into_two[h.name].at[0], h.two_dev(h.two.fwd))
        msgs.send((h.name, "two", 1), held.at[h.two.bwd], into_two[h.name].at[1], h.two_dev(h.two.bwd))

    for h in halves:
        first_total(h)

    for k in range(3):
        msgs.land(("v2", k))
    vec_all[t] = vec_sum[...] + vec_two[0] + vec_two[1] + vec_two[2]
    for k, o in enumerate(others):
        msgs.send(("v3", k), vec_all.at[t], vec_all.at[t], group_member(x, z, o))

    for h in halves:
        msgs.land((h.name, "two", 0))
        v = held_two[h.name][h.two.fwd].astype(F32) + into_two[h.name][0].astype(F32)
        last[h.name][...] = v.astype(BF)
        msgs.send((h.name, "two", 2), last[h.name], into_two[h.name].at[2], h.two_dev(h.two.fwd))

    for a, src, dst in arrays:
        msgs.land(("sib", a, 3))
        msgs.land(("y", a, 1))
        msgs.land(("y", a, 2))

        def add(r, a=a, src=src, dst=dst):
            v = src[mine(y), r, :].astype(F32) + sib[a, y, r, :].astype(F32)
            dst[r, :] = v + from_y[a, 1, r, :].astype(F32) + from_y[a, 2, r, :].astype(F32)

        slabs(256, 32, add)

    def second_total(h):
        msgs.land((h.name, "two", 1))
        msgs.land((h.name, "two", 2))
        two = into_two[h.name]
        return held_two[h.name][h.two.own].astype(F32) + two[1].astype(F32) + two[2].astype(F32)

    fin_a = m["fin_a"]
    fin_a[...] = second_total(ha).reshape(8, 8, 896)
    for k, o in enumerate(others):
        msgs.send(("n", k), fin_a.at[o], n_all.at[t], group_member(x, z, o))
    n_all[t] = fin_a[t]
    v = second_total(hb)
    own_b[0:8, :] = v[0:8]
    own_b[8:40, :] = v[16:48]
    msgs.finish()


def whole(*args):
    vmem = pl.BlockSpec(memory_space=pltpu.VMEM)
    return pl.pallas_call(
        whole_kernel,
        out_shape=(
            jax.ShapeDtypeStruct((256, 1024), F32),
            jax.ShapeDtypeStruct((256, 1024), F32),
            jax.ShapeDtypeStruct((8, 8, 896), F32),
            jax.ShapeDtypeStruct((40, 1024), F32),
            jax.ShapeDtypeStruct((8, 8, 256), F32),
            jax.ShapeDtypeStruct((8, 1024), F32),
        ),
        in_specs=[vmem] * len(args),
        out_specs=(vmem,) * 6,
        scratch_shapes=[pltpu.VMEM(*spec) for spec in SCRATCH.values()]
        + [pltpu.SemaphoreType.DMA((MESSAGES,)), pltpu.SemaphoreType.DMA((MESSAGES,))],
        compiler_params=pltpu.CompilerParams(
            collective_id=0, has_side_effects=True, vmem_limit_bytes=VMEM_LIMIT
        ),
        cost_estimate=pl.CostEstimate(flops=20_000_000_000, bytes_accessed=5_000_000, transcendentals=3_000_000),
        name="whole_block",
    )(*args)


def spread_owner(d):
    t, q = d // 16, d % 16
    return (q % 4) * 32 + (q // 4) * 8 + t


def body(tokens, segments, grad_out, ln1_gain, ln1_bias, ln2_gain, ln2_bias, w_qkv, b_qkv,
         w_dense, b_dense, w_fc1, b_fc1, w_fc2, b_fc2):
    me = lax.axis_index("fsdp")

    there = [(d, spread_owner(d)) for d in range(128)]
    back = [(b, a) for a, b in there]
    moved = lax.ppermute(jnp.concatenate([w_dense, w_fc2], 0), "fsdp", there)
    small = jnp.concatenate(
        [ln1_gain, ln1_bias, ln2_gain, ln2_bias, b_qkv, b_fc1, b_dense, b_fc2, jnp.zeros((24,), BF)]
    )
    small = jnp.broadcast_to(small.astype(F32), (8, 128))
    out_sum, g_sum, n_all, own_b, sums, b_out = whole(
        tokens, grad_out, segments, w_qkv, w_fc1, moved[0:8], moved[8:40], small, jnp.asarray(rotary_table())
    )
    grad_b = lax.ppermute(own_b, "fsdp", back)

    live = (segments.reshape(256, 1) >= 0).astype(F32)
    x = tokens.astype(F32)
    out = (x + live * (out_sum + b_out[0:1, :])).astype(BF)
    centre = x - jnp.mean(x, -1, keepdims=True)
    scale = lax.rsqrt(jnp.mean(centre * centre, -1, keepdims=True) + NORM_EPS)
    normed = centre * scale
    dx = (g_sum - jnp.mean(g_sum, -1, keepdims=True) - normed * jnp.mean(g_sum * normed, -1, keepdims=True)) * scale
    grad_tokens = (grad_out.astype(F32) + dx).astype(BF)

    sums = sums.reshape(8, 2, 1024)
    sum_qkv = sums[:, 0, 0:384].reshape(8, 3, 128).transpose(1, 0, 2).reshape(3072)
    sum_fc1 = sums[:, 0, 384:896].reshape(4096)
    n_qkv = n_all[:, :, 0:384].reshape(8, 8, 3, 128).transpose(1, 2, 0, 3).reshape(8, 3072)
    n_fc1 = n_all[:, :, 384:896].transpose(1, 0, 2).reshape(8, 4096)

    def norm_grads(weight, n, s, gain, bias_of):
        weight = weight.astype(F32)
        grad_w = gain.astype(F32)[:, None] * n + bias_of.astype(F32)[:, None] * s
        return jnp.sum(weight * n, 1), jnp.sum(weight * s, 1), grad_w

    g1_gain, g1_bias, grad_qkv = norm_grads(w_qkv, n_qkv, sum_qkv, ln1_gain, ln1_bias)
    g2_gain, g2_bias, grad_fc1 = norm_grads(w_fc1, n_fc1, sum_fc1, ln2_gain, ln2_bias)
    grad_b_qkv = lax.dynamic_slice(sum_qkv, (me * 24,), (24,))
    grad_b_fc1 = lax.dynamic_slice(sum_fc1, (me * 32,), (32,))
    grad_b_out = lax.dynamic_slice(sums[0, 1], (me * 8,), (8,))
    return (out, grad_tokens, g1_gain, g1_bias, g2_gain, g2_bias, grad_qkv, grad_b_qkv,
            grad_b[0:8], grad_b_out, grad_fc1, grad_b_fc1, grad_b[8:40], grad_b_out)


def solution(mesh):
    rows, flat = P("fsdp", None), P("fsdp")
    return jax.shard_map(
        body,
        mesh=mesh,
        in_specs=(rows, rows, rows, flat, flat, flat, flat, rows, flat, rows, flat, rows, flat, rows, flat),
        out_specs=(rows, rows, flat, flat, flat, flat, rows, flat, rows, flat, rows, flat, rows, flat),
        check_vma=False,
    )
```

time: 216 us -> 146 us (0.68)
  the two profiles are of different devices: /device:TPU:1 before, /device:TPU:6 now
where the time goes in v2:
time: 146 us; the launch traced here: 145 us
  Pallas kernels  110 us (75%)
  local copies, waits for them, and re-layouts  12.5 us (9%)
  starting transfers between devices  8.31 us (6%)
  other arithmetic  8.24 us (6%)
  waiting for transfers between devices  5.48 us (4%)
    pallas_call x1, Pallas kernels, whole(): pl.pallas_call(whole_kernel, out_shape=(jax.ShapeDtypeStruct((256, 1024),...  110 us
    ppermute x1, waiting for transfers between devices, body(): grad_b = lax.ppermute(own_b, 'fsdp', back)  5.48 us
    ppermute x1, starting transfers between devices, body(): moved = lax.ppermute(jnp.concatenate([w_dense, w_fc2], 0), 'fsdp', there)  4.83 us
    unnamed x36, local copies, waits for them, and re-layouts  4.49 us
    ppermute x1, starting transfers between devices, body(): grad_b = lax.ppermute(own_b, 'fsdp', back)  3.48 us
  transfers between devices with their start and end apart: 2, of which 1 were waited for; matrix products, arithmetic and copies ran while one was open for 6% of the time, Pallas kernels for 0%

profile of v2, /device:TPU:6, one launch (start us, length us, event | category | flops | bytes accessed | tf_op | source)
XLA Modules:
  0.0 145.1 jit_solution(6362498288941953255)
XLA Ops:
  0.6 0.0 copy-start
  0.7 0.9 pad_maximum_fusion
  1.6 4.8 %collective-permute-start = (bf16[40,1024]{1,0:T(8,128)(2,1)S(1)}, bf16[40,1024]{1,0:T(8,128)(2,1)S(1)}, u32[]{:S(2)}, u32[]{:S(2)}) collective-permute-start(bf16[40,1024]{1,0:T(8,128)(2,1)S(1)} %pad_maximum_fusion), channel_id=1, source_target_pairs={{0,0},{1,32},{2,64},{3,96},{4,8},{5,40},{6,72},{7,104},{8,16},{9,4... | collective-permute-start | bytes 245768 | tf_op jit(solution)/shard_map/ppermute | solution.py:665
  6.4 1.2 convert_reduce_fusion
  7.6 0.0 copy-done
  7.6 0.3 fusion.9
  7.9 0.0 copy-start.7
  7.9 0.7 copy-done.7
  8.6 0.0 copy-start.10
  8.6 0.7 copy-done.10
  9.2 0.6 copy-done.11
  9.9 0.7 copy-done.8
  10.5 0.7 copy-done.9
  11.2 0.0 copy-done.15
  11.2 0.6 copy-done.12
  11.9 0.0 copy-done.13
  11.9 0.0 copy-done.14
  11.9 0.1 concatenate.7
  12.0 0.0 collective-permute-done
  12.0 0.6 slice.41.fc2_ref
  12.6 0.6 slice.40.dense_ref
  13.2 0.6 broadcast_in_dim.2.small_ref
  13.8 109.7 %whole_block.1 = (f32[256,1024]{1,0:T(8,128)}, f32[256,1024]{1,0:T(8,128)}, f32[8,8,896]{2,1,0:T(8,128)}, f32[40,1024]{1,0:T(8,128)}, f32[8,8,256]{2,1,0:T(8,128)}, /*index=5*/f32[8,1024]{1,0:T(8,128)}) custom-call(bf16[256,1024]{1,0:T(8,128)(2,1)} %x_ref.1, bf16[256,1024]{1,0:T(8,128)(2,1)} %dy_ref.1, s32[2,128]{1,0:T(2,128)} %seg_ref.1, ...), custom_call_target="tpu_custom_call" | custom-call | flops 20000000000 | bytes 5000000 | tf_op jit(solution)/shard_map/whole_block/pallas_call | solution.py:632
  123.5 0.0 copy-start.1
  123.6 0.0 copy-start.5
  123.6 0.9 reshape.84
  124.6 0.9 slice.35
  125.5 0.9 slice_bitcast_fusion
  126.4 0.8 slice.32
  127.2 0.1 dynamic-slice_bitcast_fusion
  127.2 3.5 %collective-permute-start.1 = (f32[40,1024]{1,0:T(8,128)}, f32[40,1024]{1,0:T(8,128)S(1)}, u32[]{:S(2)}, u32[]{:S(2)}) collective-permute-start(f32[40,1024]{1,0:T(8,128)} %get-tuple-element.25), channel_id=1, source_target_pairs={{0,0},{32,1},{64,2},{96,3},{8,4},{40,5},{72,6},{104,7},{16,8},{48,... | collective-permute-start | bytes 491528 | tf_op jit(solution)/shard_map/ppermute | solution.py:673
  130.7 0.0 copy-done.1
  130.7 1.6 %fusion.16 = (f32[256]{0:T(256)S(1)}, f32[256]{0:T(256)S(1)}) fusion(f32[256,1024]{1,0:T(8,128)} %get-tuple-element.22, f32[256]{0:T(256)S(1)} %add_rsqrt_fusion, f32[256]{0:T(256)S(1)} %broadcast_multiply_fusion.1, bf16[256,1024]{1,0:T(8,128)(2,1)S(1)} %copy-done.1), kind=kLoop, calls=%fused_computation.34 | loop fusion | flops 1572352 | bytes 1576960 | tf_op jit(solution)/shard_map/reduce_sum | solution.py:681
  132.3 0.6 dynamic_slice.11
  132.9 0.6 dynamic_slice.14
  133.5 0.0 copy-done.5
  133.5 1.4 fusion.12
  134.9 0.0 copy-done.4
  134.9 0.0 copy-done.2
  134.9 0.0 copy-done.3
  134.9 1.5 %fusion.8 = (bf16[256,1024]{1,0:T(8,128)(2,1)}, bf16[256,1024]{1,0:T(8,128)(2,1)}) fusion(bf16[256,1024]{1,0:T(8,128)(2,1)S(1)} %copy-done.1, f32[256,1024]{1,0:T(8,128)S(1)} %copy-done.2, bf16[256,1024]{1,0:T(8,128)(2,1)S(1)} %copy-done.4, f32[256]{0:T(256)S(1)} %get-tuple-element.36, f32[256]{0:T(256)S(1)} %add_rsqrt_fusion, ...), kind=kLoop, calls=%fused_computation.11 | loop fusion | flops 3670016 | bytes 4203520 | tf_op jit(solution)/shard_map/convert_element_type | solution.py:682
  136.4 0.0 copy-done.6
  136.4 1.4 fusion.14
  137.8 5.5 %collective-permute-done.1 = f32[40,1024]{1,0:T(8,128)S(1)} collective-permute-done((f32[40,1024]{1,0:T(8,128)}, f32[40,1024]{1,0:T(8,128)S(1)}, u32[]{:S(2)}, u32[]{:S(2)}) %collective-permute-start.1) | collective-permute-done | bytes 163872 | tf_op jit(solution)/shard_map/ppermute | solution.py:673
  143.3 0.7 slice.46
  143.9 0.6 slice.44
  144.5 0.0 copy-done.16
  144.5 0.5 copy.37
  (26 shorter events, 0.1 us)
Async XLA Ops:
  0.6 7.0 %copy-start = (bf16[256,1024]{1,0:T(8,128)(2,1)S(1)}, bf16[256,1024]{1,0:T(8,128)(2,1)}, u32[]{:S(2)}) copy-start(bf16[256,1024]{1,0:T(8,128)(2,1)} %x_ref.1) | copy-start | bytes 1572868
  1.6 10.4 %collective-permute-start = (bf16[40,1024]{1,0:T(8,128)(2,1)S(1)}, bf16[40,1024]{1,0:T(8,128)(2,1)S(1)}, u32[]{:S(2)}, u32[]{:S(2)}) collective-permute-start(bf16[40,1024]{1,0:T(8,128)(2,1)S(1)} %pad_maximum_fusion), channel_id=1, source_target_pairs={{0,0},{1,32},{2,64},{3,96},{4,8},{5,40},{6,72},{7,104},{8,16},{9,4... | collective-permute-start | bytes 245768 | tf_op jit(solution)/shard_map/ppermute | solution.py:665
  7.9 0.7 copy-start.7
  8.6 0.7 copy-start.10
  9.2 0.7 copy-start.11
  9.2 2.0 %copy-start.15 = (bf16[8]{0:T(256)(128)(2,1)S(1)}, bf16[8]{0:T(256)(128)(2,1)}, u32[]{:S(2)}) copy-start(bf16[8]{0:T(256)(128)(2,1)} %param.30) | copy-start | bytes 52
  9.9 0.7 copy-start.8
  10.5 0.7 copy-start.9
  11.2 0.7 copy-start.12
  11.2 0.7 copy-start.13
  11.2 0.7 copy-start.14
  13.8 121.1 %copy-start.4 = (bf16[256,1024]{1,0:T(8,128)(2,1)S(1)}, bf16[256,1024]{1,0:T(8,128)(2,1)}, u32[]{:S(2)}) copy-start(bf16[256,1024]{1,0:T(8,128)(2,1)} %dy_ref.1) | copy-start | bytes 1572868
  123.5 7.2 %copy-start.1 = (bf16[256,1024]{1,0:T(8,128)(2,1)S(1)}, bf16[256,1024]{1,0:T(8,128)(2,1)}, u32[]{:S(2)}) copy-start(bf16[256,1024]{1,0:T(8,128)(2,1)} %x_ref.1) | copy-start | bytes 1572868
  123.6 9.9 %copy-start.5 = (bf16[8,4096]{1,0:T(8,128)(2,1)S(1)}, bf16[8,4096]{1,0:T(8,128)(2,1)}, u32[]{:S(2)}) copy-start(bf16[8,4096]{1,0:T(8,128)(2,1)} %wfc1_ref.1) | copy-start | bytes 196612
  127.2 17.3 %copy-start.16 = (f32[8]{0:T(128)}, f32[8]{0:T(128)S(1)}, u32[]{:S(2)}) copy-start(f32[8]{0:T(128)S(1)} %dynamic-slice_bitcast_fusion) | copy-start | bytes 100
  127.2 7.7 %copy-start.2 = (f32[256,1024]{1,0:T(8,128)S(1)}, f32[256,1024]{1,0:T(8,128)}, u32[]{:S(2)}) copy-start(f32[256,1024]{1,0:T(8,128)} %get-tuple-element.22) | copy-start | bytes 3145732
  127.2 7.7 %copy-start.3 = (f32[256,1024]{1,0:T(8,128)S(1)}, f32[256,1024]{1,0:T(8,128)}, u32[]{:S(2)}) copy-start(f32[256,1024]{1,0:T(8,128)} %get-tuple-element.20) | copy-start | bytes 3145732
  127.2 16.0 %collective-permute-start.1 = (f32[40,1024]{1,0:T(8,128)}, f32[40,1024]{1,0:T(8,128)S(1)}, u32[]{:S(2)}, u32[]{:S(2)}) collective-permute-start(f32[40,1024]{1,0:T(8,128)} %get-tuple-element.25), channel_id=1, source_target_pairs={{0,0},{32,1},{64,2},{96,3},{8,4},{40,5},{72,6},{104,7},{16,8},{48,... | collective-permute-start | bytes 491528 | tf_op jit(solution)/shard_map/ppermute | solution.py:673
  134.9 1.5 %copy-start.6 = (bf16[8,3072]{1,0:T(8,128)(2,1)S(1)}, bf16[8,3072]{1,0:T(8,128)(2,1)}, u32[]{:S(2)}) copy-start(bf16[8,3072]{1,0:T(8,128)(2,1)} %wqkv_ref.1) | copy-start | bytes 147460

commit v3 on v2

--- a/solution.py
+++ b/solution.py
@@ -42,9 +42,9 @@
 class Messages:
     def __init__(self, send_sem, recv_sem):
         self.send_sem, self.recv_sem = send_sem, recv_sem
-        self.sent, self.landed = {}, set()
-
-    def plan(self, name, src, dst, target):
+        self.sent, self.landed, self.apart = {}, set(), set()
+
+    def plan(self, name, src, dst, target, apart=False):
         n = len(self.sent)
         copy = pltpu.make_async_remote_copy(
             src_ref=src,
@@ -55,6 +55,8 @@
             device_id_type=MESH,
         )
         self.sent[name] = copy
+        if apart:
+            self.apart.add(name)
 
     def send(self, name, src, dst, target):
         self.plan(name, src, dst, target)
@@ -67,17 +69,11 @@
 
     def finish(self):
         for name, copy in self.sent.items():
-            if name not in self.landed:
+            if name not in self.landed and name not in self.apart:
                 copy.wait_recv()
-        for copy in self.sent.values():
-            copy.wait_send()
-
-
-def enter(targets):
-    barrier = pltpu.get_barrier_semaphore()
-    for target in targets:
-        pl.semaphore_signal(barrier, inc=1, device_id=(target,), device_id_type=MESH)
-    pl.semaphore_wait(barrier, len(targets))
+        for name, copy in self.sent.items():
+            if name not in self.apart:
+                copy.wait_send()
 
 
 def group_member(x, z, t):
@@ -150,7 +146,7 @@
     qkv_at = lambda at: (at >> 7) * 1024 + t * 128 + (at & 127)
     d24 = lambda c: (c * 2731) >> 16
     b_qkv = pick(384, lambda at: [32 + qkv_at(at) - 24 * d24(qkv_at(at))], lambda at: d24(qkv_at(at)))
-    b_fc1 = pick(512, lambda at: [56 + (at & 31)], lambda at: t * 16 + (at >> 5))
+    b_fc1 = pick(512, lambda at: [56 + (at & 31)], lambda at: ((at >> 5) & 3) * 32 + (at >> 7) * 8 + t)
     return ln, b_qkv, b_fc1, b_out
 
 
@@ -172,7 +168,7 @@
     col = lax.broadcasted_iota(jnp.int32, (128, 128), 1)
     masks, lives, tables = [], [], []
     for b in range(2):
-        seg_c = jnp.broadcast_to(seg[b : b + 1, :].astype(F32), (128, 128))
+        seg_c = jnp.broadcast_to(seg[b : b + 1, :], (128, 128))
         seg_r = seg_c.T
         allowed = (seg_c == seg_r) & (col <= row)
         position = jnp.sum(allowed.astype(F32), 1, keepdims=True) - 1.0
@@ -194,6 +190,7 @@
         zero = jnp.zeros_like(u)
         return jnp.concatenate([jnp.where(head0, u, zero), jnp.where(head0, zero, u)], 0)
 
+    ones = jnp.ones((128, 128), BF)
     contexts, d_joined = [], []
     for b in range(2):
         part = slice(b * 128, b * 128 + 128)
@@ -206,9 +203,11 @@
         allowed = jnp.concatenate([masks[b], masks[b]], 0)
         scores = jnp.where(allowed, dot_nt(q2, k) * 0.125, MASKED)
         e = jnp.exp(scores - jnp.max(scores, 1, keepdims=True))
-        probs = e / jnp.sum(e, 1, keepdims=True)
+        ctx = dot(e.astype(BF), jnp.concatenate([v, ones], 1))
+        inverse = 1.0 / ctx[:, 128:256]
+        probs = e * inverse
         probs_b = probs.astype(BF)
-        ctx = dot(probs_b, v)
+        ctx = ctx[:, 0:128] * inverse
         ctx = jnp.where(head0, ctx[0:128], ctx[128:256]).astype(BF).astype(F32)
         contexts.append((ctx * lives[b]).astype(BF))
         dc2 = stacked(d_context[part])
@@ -236,9 +235,14 @@
 SCRATCH = dict(
     X=((8, 256, 1024), BF),
     DY=((8, 256, 1024), BF),
-    SEG=((8, 2, 128), jnp.int32),
-    SM=((8, 8, 128), F32),
-    AW=((8, 8, 896), BF),
+    qkv=((8, 3072), BF),
+    fc1=((8, 4096), BF),
+    small=((8, 128), BF),
+    table=((128, 512), BF),
+    dense=((8, 1024), BF),
+    fc2=((32, 1024), BF),
+    stage=((8, 8, 1024), BF),
+    AW=((8, 8, 1024), BF),
     WA=((4, 4, 64, 896), BF),
     WB=((4, 4, 48, 1024), BF),
     w1=((1024, 896), BF),
@@ -261,24 +265,23 @@
     held_one_b=((4, 48, 1024), BF),
     two_a=((3, 64, 896), BF),
     two_b=((3, 48, 1024), BF),
-    held_two_a=((4, 64, 896), BF),
-    held_two_b=((4, 48, 1024), BF),
-    last_a=((64, 896), BF),
-    last_b=((48, 1024), BF),
+    held_two_a=((3, 64, 896), BF),
+    held_two_b=((3, 48, 1024), BF),
     fin_a=((8, 8, 896), F32),
+    own_dense=((8, 1024), F32),
     vec=((8, 256), F32),
     vec_one=((3, 8, 256), F32),
     vec_sum=((8, 256), F32),
     vec_two=((3, 8, 256), F32),
 )
-MESSAGES = 7 * 6 + 2 * 7 + 2 * (3 + 12) + 13 + 2 * (4 + 3) + 2 * 6 + 7
-
-
-def whole_kernel(x_ref, dy_ref, seg_ref, wqkv_ref, wfc1_ref, dense_ref, fc2_ref, small_ref, table_ref,
-                 out_sum, g_sum, n_all, own_b, vec_all, b_out, *scratch):
+MESSAGES = 7 + 1 + 2 * 7 + 2 * (3 + 12) + 13 + 2 * (4 + 3) + 2 * (12 + 3) + 7 + 1
+
+
+def whole_kernel(x_ref, dy_ref, wqkv_ref, wfc1_ref, dense_ref, fc2_ref, small_ref, table_hbm,
+                 out_sum, g_sum, n_all, grad_dense, grad_fc2, vec_all, b_out, *scratch):
     m = dict(zip(SCRATCH, scratch))
-    send_sem, recv_sem = scratch[len(SCRATCH) :]
-    X, DY, SEG, SM, AW, WA, WB = (m[k] for k in ("X", "DY", "SEG", "SM", "AW", "WA", "WB"))
+    send_sem, recv_sem, local_sem = scratch[len(SCRATCH) :]
+    X, DY, AW, WA, WB, stage, table_ref = (m[k] for k in ("X", "DY", "AW", "WA", "WB", "stage", "table"))
     x, z, y, core = coords()
     t = y * 2 + core
     ring_y, ring_x, ring_z = Ring(y, core), Ring(x, core), Ring(z, core)
@@ -295,49 +298,100 @@
         Half("a", ring_x, x_dev, ring_z, z_dev, 64),
         Half("b", ring_z, z_dev, ring_x, x_dev, 48),
     )
-    enter([group_member(x, z, o) for o in others] + [x_dev(o) for o in x_others] + [z_dev(o) for o in z_others])
+    owner = t * 16 + z * 4 + x
+    me = ident(x, z, y, core)
+    spreader = ident(lax.rem(me, 4), lax.rem(me // 4, 4), 0, 0) + me // 16
+    moves = spreader != me
+
+    local = [
+        pltpu.make_async_copy(src, dst, local_sem.at[n])
+        for n, (src, dst) in enumerate(
+            (
+                (wqkv_ref, m["qkv"]),
+                (wfc1_ref, m["fc1"]),
+                (small_ref, m["small"]),
+                (fc2_ref, m["fc2"]),
+                (table_hbm, table_ref),
+                (x_ref, X.at[t]),
+                (dy_ref, DY.at[t]),
+            )
+        )
+    ]
+    for copy in local:
+        copy.start()
+    barrier = pltpu.get_barrier_semaphore()
+    near = [group_member(x, z, o) for o in others] + [x_dev(o) for o in x_others] + [z_dev(o) for o in z_others]
+    for target in near:
+        pl.semaphore_signal(barrier, inc=1, device_id=(target,), device_id_type=MESH)
+
+    @pl.when(moves)
+    def _():
+        for target in (owner, spreader):
+            pl.semaphore_signal(barrier, inc=1, device_id=(target,), device_id_type=MESH)
+
+    for copy in local[:4]:
+        copy.wait()
+    fc1_rows = m["fc1"][...].astype(F32)
+    for o in range(8):
+        for sec in range(3):
+            stage[o, :, sec * 128 : sec * 128 + 128] = m["qkv"][:, sec * 1024 + o * 128 : sec * 1024 + o * 128 + 128]
+        columns = [fc1_rows[:, at : at + 32] for at in [p * 1024 + q * 256 + o * 32 for q in range(4) for p in range(4)]]
+        stage[o, :, 384:896] = jnp.concatenate(columns, 1).astype(BF)
+        stage[o, :, 896:1024] = m["small"][...]
+
+    @pl.when(moves)
+    def _():
+        pl.semaphore_wait(barrier, len(near) + 2)
+
+    @pl.when(jnp.logical_not(moves))
+    def _():
+        pl.semaphore_wait(barrier, len(near))
+
     msgs = Messages(send_sem, recv_sem)
 
     for k, o in enumerate(others):
-        dev = group_member(x, z, o)
-        for sec in range(3):
-            lanes = pl.ds(pl.multiple_of(sec * 1024 + o * 128, 128), 128)
-            msgs.send(("w", k, sec), wqkv_ref.at[:, lanes], AW.at[t, :, pl.ds(sec * 128, 128)], dev)
-        lanes = pl.ds(pl.multiple_of(o * 512, 512), 512)
-        msgs.send(("w", k, 3), wfc1_ref.at[:, lanes], AW.at[t, :, pl.ds(384, 512)], dev)
-        msgs.send(("w", k, 4), small_ref, SM.at[t], dev)
-    rows = (("x", x_ref, X), ("d", dy_ref, DY))
+        msgs.send(("w", k), stage.at[o], AW.at[t], group_member(x, z, o))
+    lone = pltpu.make_async_copy(dense_ref, m["dense"], local_sem.at[7])
+    msgs.plan("there", dense_ref, m["dense"], spreader, apart=True)
+    msgs.plan("back", m["own_dense"], grad_dense, owner, apart=True)
+
+    @pl.when(moves)
+    def _():
+        msgs.sent["there"].start()
+
+    @pl.when(jnp.logical_not(moves))
+    def _():
+        lone.start()
 
     def own_rows(name, src, dst):
         msgs.send((name, 0), src, dst.at[t], y_dev(ring_y.fwd))
         msgs.send((name, 1), src, dst.at[t], y_dev(ring_y.bwd))
         msgs.send((name, 2), src, dst.at[t], sibling)
 
-    own_rows(*rows[0])
-    for k, o in enumerate(others):
-        msgs.send(("s", k), seg_ref, SEG.at[t], group_member(x, z, o))
-    own_rows(*rows[1])
-    for sec in range(3):
-        lanes = pl.ds(pl.multiple_of(sec * 1024 + t * 128, 128), 128)
-        AW[t, :, sec * 128 : sec * 128 + 128] = wqkv_ref[:, lanes]
-    AW[t, :, 384:896] = wfc1_ref[:, pl.ds(pl.multiple_of(t * 512, 512), 512)]
-    SM[t] = small_ref[...]
-    X[t] = x_ref[...]
-    DY[t] = dy_ref[...]
-    SEG[t] = seg_ref[...]
+    own_rows("x", x_ref, X)
+    own_rows("d", dy_ref, DY)
+    AW[t] = stage[t]
     for k in range(7):
-        for sec in range(5):
-            msgs.land(("w", k, sec))
+        msgs.land(("w", k))
     for pair in range(4):
         both = jnp.concatenate([AW[2 * pair].astype(F32), AW[2 * pair + 1].astype(F32)], 0)
-        WA[x, z, 16 * pair : 16 * pair + 16, :] = both.astype(BF)
+        WA[x, z, 16 * pair : 16 * pair + 16, :] = both[:, 0:896].astype(BF)
+
+    @pl.when(moves)
+    def _():
+        msgs.sent["there"].wait_recv()
+
+    @pl.when(jnp.logical_not(moves))
+    def _():
+        lone.wait()
+
     member = lax.broadcasted_iota(jnp.int32, (8, 128), 0)
     small = jnp.zeros((8, 128), F32)
     for k in range(8):
-        small = jnp.where(member == k, SM[k], small)
+        small = jnp.where(member == k, AW[k, :, 896:1024].astype(F32)[0:1], small)
     small = jnp.concatenate([small, jnp.zeros((8, 896), F32)], 1)
-    WB[z, x, 0:16, :] = jnp.concatenate([dense_ref[...].astype(F32), small], 0).astype(BF)
-    WB[z, x, 16:48, :] = fc2_ref[...]
+    WB[z, x, 0:16, :] = jnp.concatenate([m["dense"][...].astype(F32), small], 0).astype(BF)
+    WB[z, x, 16:48, :] = m["fc2"][...]
 
     gathered = {"a": WA, "b": WB}
 
@@ -378,29 +432,28 @@
     def rows_on(name, dst):
         msgs.land((name, 0))
         ref = dst.at[mine(ring_y.bwd)]
-        msgs.send((name, 3), ref, ref, y_dev(ring_y.fwd))
         msgs.send((name, 4), ref, ref, sibling)
         msgs.land((name, 1))
         ref = dst.at[mine(ring_y.fwd)]
         msgs.send((name, 5), ref, ref, sibling)
 
-    def rows_last(name, dst):
-        msgs.land((name, 3))
-        ref = dst.at[mine(ring_y.opp)]
-        msgs.send((name, 6), ref, ref, sibling)
+    def rows_far(name, dst):
+        ref = dst.at[mine(ring_y.bwd)]
+        msgs.send((name, 3), ref, ref, y_dev(ring_y.fwd))
 
     rows_on("x", X)
     for sub in ("bwd", "fwd", "opp"):
         for h in halves:
             pass_on(h, sub)
     rows_on("d", DY)
-    rows_last("x", X)
-    for k in range(7):
-        msgs.land(("s", k))
+    rows_far("x", X)
+    rows_far("d", DY)
     for h in halves:
         for sub in ("own", "bwd", "fwd", "opp"):
             msgs.land((h.name, sub, 1))
             msgs.land((h.name, sub, 2))
+    for copy in local[4:]:
+        copy.wait()
 
     w1, w2, ln, bias = m["w1"], m["w2"], m["ln"], m["bias"]
     w1[...] = WA[...].reshape(1024, 896)
@@ -429,8 +482,9 @@
 
         slabs(256, 32, add)
 
-    ref = DY.at[mine(ring_y.opp)]
-    msgs.plan(("d", 6), ref, ref, sibling)
+    for name, dst in (("x", X), ("d", DY)):
+        ref = dst.at[mine(ring_y.opp)]
+        msgs.plan((name, 6), ref, ref, sibling)
     for a, src, _ in arrays:
         for k in range(4):
             msgs.plan(("sib", a, k), src.at[hers(chips[k])], sib.at[a, chips[k]], sibling)
@@ -444,10 +498,14 @@
                 msgs.land((name, 4))
                 msgs.land((name, 5))
 
+        @pl.when(s == 2)
+        def _():
+            for name in "xd":
+                msgs.land((name, 3))
+                msgs.sent[name, 6].start()
+
         @pl.when(s == 4)
         def _():
-            msgs.land(("d", 3))
-            msgs.sent["d", 6].start()
             msgs.land(("x", 6))
             msgs.land(("d", 6))
 
@@ -485,7 +543,7 @@
         chip = jnp.where(k == 0, chips[0], jnp.where(k == 1, chips[1], jnp.where(k == 2, chips[2], chips[3])))
         slot = chip * 2 + jnp.where(s % 2 == 0, 1 - core, core)
         out, g, normed, d_all, cat, column_sums = rows_pass(
-            X[slot], DY[slot], SEG[slot], w1, w2, ln, bias, table_ref
+            X[slot], DY[slot], AW[slot][:, 896:1024].astype(F32)[1:3], w1, w2, ln, bias, table_ref
         )
         OUT[slot] = out.astype(BF)
         G[slot] = g.astype(BF)
@@ -510,7 +568,6 @@
     held_one = {"a": m["held_one_a"], "b": m["held_one_b"]}
     into_two = {"a": m["two_a"], "b": m["two_b"]}
     held_two = {"a": m["held_two_a"], "b": m["held_two_b"]}
-    last = {"a": m["last_a"], "b": m["last_b"]}
     ha, hb = halves
 
     def grad_a(at):
@@ -527,8 +584,38 @@
         part["b"][first_at, :, 16:48, :] = v[0:128].reshape(4, 32, 1024).astype(BF)
         part["b"][second_at, :, 16:48, :] = v[128:256].reshape(4, 32, 1024).astype(BF)
 
+    subs = ("opp", "bwd", "fwd", "own")
+
     def send_one(h, k, at, to):
-        msgs.send((h.name, "one", k), part[h.name].at[at], into_one[h.name].at[k], h.one_dev(to))
+        for sub in subs:
+            j = getattr(h.two, sub)
+            msgs.send((h.name, "one", k, sub), part[h.name].at[at, j], into_one[h.name].at[k, j], h.one_dev(to))
+
+    def send_forward(h, sub):
+        j = getattr(h.two, sub)
+        msgs.land((h.name, "one", 0, sub))
+        v = part[h.name][h.one.fwd, j].astype(F32) + into_one[h.name][0, j].astype(F32)
+        held_one[h.name][j] = v.astype(BF)
+        msgs.send((h.name, "one", 2, sub), held_one[h.name].at[j], into_one[h.name].at[2, j], h.one_dev(h.one.fwd))
+
+    def first_sum(h, sub):
+        j = getattr(h.two, sub)
+        msgs.land((h.name, "one", 1, sub))
+        msgs.land((h.name, "one", 2, sub))
+        v = part[h.name][h.one.own, j].astype(F32) + into_one[h.name][1, j].astype(F32)
+        v = v + into_one[h.name][2, j].astype(F32)
+        k = subs.index(sub)
+        if sub == "fwd":
+            msgs.land((h.name, "two", 0))
+            v = v + into_two[h.name][0].astype(F32)
+        if sub != "own":
+            held_two[h.name][k] = v.astype(BF)
+            to = h.two.bwd if sub == "bwd" else h.two.fwd
+            msgs.send((h.name, "two", k), held_two[h.name].at[k], into_two[h.name].at[k], h.two_dev(to))
+            return None
+        msgs.land((h.name, "two", 1))
+        msgs.land((h.name, "two", 2))
+        return v + into_two[h.name][1].astype(F32) + into_two[h.name][2].astype(F32)
 
     v = dot_tn(CAT[:, :, 0:128].reshape(2048, 128), DY[...].reshape(2048, 1024)).reshape(4, 4, 8, 1024)
     part["b"][:, :, 0:16, :] = jnp.concatenate([v, jnp.zeros_like(v)], 2).astype(BF)
@@ -546,7 +633,12 @@
     grad_a(ring_x.bwd)
     send_one(ha, 1, ring_x.bwd, ring_x.bwd)
     grad_a(ring_x.fwd)
+    for sub in subs:
+        send_forward(ha, sub)
     grad_b(ring_z.fwd, ring_z.own)
+    for sub in subs:
+        send_forward(hb, sub)
+    grad_a(ring_x.own)
 
     for k in range(3):
         msgs.land(("v1", k))
@@ -554,38 +646,9 @@
     for k, o in enumerate(z_others):
         msgs.send(("v2", k), vec_sum, vec_two.at[k], z_dev(o))
 
-    def slab_of(h):
-        return h.rows // (4 if h.name == "a" else 3)
-
-    def first_forward(h):
-        msgs.land((h.name, "one", 0))
-
-        def add(r):
-            v = part[h.name][h.one.fwd, :, r, :].astype(F32) + into_one[h.name][0, :, r, :].astype(F32)
-            held_one[h.name][:, r, :] = v.astype(BF)
-
-        slabs(h.rows, slab_of(h), add)
-        msgs.send((h.name, "one", 2), held_one[h.name], into_one[h.name].at[2], h.one_dev(h.one.fwd))
-
-    for h in halves:
-        first_forward(h)
-    grad_a(ring_x.own)
-
-    def first_total(h):
-        msgs.land((h.name, "one", 1))
-        msgs.land((h.name, "one", 2))
-
-        def add(r):
-            v = part[h.name][h.one.own, :, r, :].astype(F32) + into_one[h.name][1, :, r, :].astype(F32)
-            held_two[h.name][:, r, :] = (v + into_one[h.name][2, :, r, :].astype(F32)).astype(BF)
-
-        slabs(h.rows, slab_of(h), add)
-        held = held_two[h.name]
-        msgs.send((h.name, "two", 0), held.at[h.two.opp], into_two[h.name].at[0], h.two_dev(h.two.fwd))
-        msgs.send((h.name, "two", 1), held.at[h.two.bwd], into_two[h.name].at[1], h.two_dev(h.two.bwd))
-
-    for h in halves:
-        first_total(h)
+    for sub in ("opp", "bwd"):
+        for h in halves:
+            first_sum(h, sub)
 
     for k in range(3):
         msgs.land(("v2", k))
@@ -594,10 +657,7 @@
         msgs.send(("v3", k), vec_all.at[t], vec_all.at[t], group_member(x, z, o))
 
     for h in halves:
-        msgs.land((h.name, "two", 0))
-        v = held_two[h.name][h.two.fwd].astype(F32) + into_two[h.name][0].astype(F32)
-        last[h.name][...] = v.astype(BF)
-        msgs.send((h.name, "two", 2), last[h.name], into_two[h.name].at[2], h.two_dev(h.two.fwd))
+        first_sum(h, "fwd")
 
     for a, src, dst in arrays:
         msgs.land(("sib", a, 3))
@@ -610,39 +670,46 @@
 
         slabs(256, 32, add)
 
-    def second_total(h):
-        msgs.land((h.name, "two", 1))
-        msgs.land((h.name, "two", 2))
-        two = into_two[h.name]
-        return held_two[h.name][h.two.own].astype(F32) + two[1].astype(F32) + two[2].astype(F32)
-
     fin_a = m["fin_a"]
-    fin_a[...] = second_total(ha).reshape(8, 8, 896)
+    fin_a[...] = first_sum(ha, "own").reshape(8, 8, 896)
     for k, o in enumerate(others):
         msgs.send(("n", k), fin_a.at[o], n_all.at[t], group_member(x, z, o))
     n_all[t] = fin_a[t]
-    v = second_total(hb)
-    own_b[0:8, :] = v[0:8]
-    own_b[8:40, :] = v[16:48]
+    v = first_sum(hb, "own")
+    m["own_dense"][...] = v[0:8]
+    grad_fc2[...] = v[16:48]
+
+    @pl.when(moves)
+    def _():
+        msgs.sent["back"].start()
+        msgs.sent["there"].wait_send()
+        msgs.sent["back"].wait()
+
+    @pl.when(jnp.logical_not(moves))
+    def _():
+        grad_dense[...] = m["own_dense"][...]
+
     msgs.finish()
 
 
 def whole(*args):
     vmem = pl.BlockSpec(memory_space=pltpu.VMEM)
+    hbm = pl.BlockSpec(memory_space=pl.ANY)
     return pl.pallas_call(
         whole_kernel,
         out_shape=(
             jax.ShapeDtypeStruct((256, 1024), F32),
             jax.ShapeDtypeStruct((256, 1024), F32),
             jax.ShapeDtypeStruct((8, 8, 896), F32),
-            jax.ShapeDtypeStruct((40, 1024), F32),
+            jax.ShapeDtypeStruct((8, 1024), F32),
+            jax.ShapeDtypeStruct((32, 1024), F32),
             jax.ShapeDtypeStruct((8, 8, 256), F32),
             jax.ShapeDtypeStruct((8, 1024), F32),
         ),
-        in_specs=[vmem] * len(args),
-        out_specs=(vmem,) * 6,
+        in_specs=[hbm] * len(args),
+        out_specs=(vmem,) * 7,
         scratch_shapes=[pltpu.VMEM(*spec) for spec in SCRATCH.values()]
-        + [pltpu.SemaphoreType.DMA((MESSAGES,)), pltpu.SemaphoreType.DMA((MESSAGES,))],
+        + [pltpu.SemaphoreType.DMA((MESSAGES,)), pltpu.SemaphoreType.DMA((MESSAGES,)), pltpu.SemaphoreType.DMA((8,))],
         compiler_params=pltpu.CompilerParams(
             collective_id=0, has_side_effects=True, vmem_limit_bytes=VMEM_LIMIT
         ),
@@ -651,26 +718,18 @@
     )(*args)
 
 
-def spread_owner(d):
-    t, q = d // 16, d % 16
-    return (q % 4) * 32 + (q // 4) * 8 + t
-
-
 def body(tokens, segments, grad_out, ln1_gain, ln1_bias, ln2_gain, ln2_bias, w_qkv, b_qkv,
          w_dense, b_dense, w_fc1, b_fc1, w_fc2, b_fc2):
     me = lax.axis_index("fsdp")
 
-    there = [(d, spread_owner(d)) for d in range(128)]
-    back = [(b, a) for a, b in there]
-    moved = lax.ppermute(jnp.concatenate([w_dense, w_fc2], 0), "fsdp", there)
-    small = jnp.concatenate(
-        [ln1_gain, ln1_bias, ln2_gain, ln2_bias, b_qkv, b_fc1, b_dense, b_fc2, jnp.zeros((24,), BF)]
+    small = jnp.pad(segments.astype(BF), ((1, 5), (0, 0)))
+    at = 0
+    for vector in (ln1_gain, ln1_bias, ln2_gain, ln2_bias, b_qkv, b_fc1, b_dense, b_fc2):
+        small = small + jnp.pad(vector[None], ((0, 7), (at, 128 - at - vector.shape[0])))
+        at += vector.shape[0]
+    out_sum, g_sum, n_all, grad_dense, grad_fc2, sums, b_out = whole(
+        tokens, grad_out, w_qkv, w_fc1, w_dense, w_fc2, small, jnp.asarray(rotary_table())
     )
-    small = jnp.broadcast_to(small.astype(F32), (8, 128))
-    out_sum, g_sum, n_all, own_b, sums, b_out = whole(
-        tokens, grad_out, segments, w_qkv, w_fc1, moved[0:8], moved[8:40], small, jnp.asarray(rotary_table())
-    )
-    grad_b = lax.ppermute(own_b, "fsdp", back)
 
     live = (segments.reshape(256, 1) >= 0).astype(F32)
     x = tokens.astype(F32)
@@ -683,9 +742,9 @@
 
     sums = sums.reshape(8, 2, 1024)
     sum_qkv = sums[:, 0, 0:384].reshape(8, 3, 128).transpose(1, 0, 2).reshape(3072)
-    sum_fc1 = sums[:, 0, 384:896].reshape(4096)
+    sum_fc1 = sums[:, 0, 384:896].reshape(8, 4, 4, 32).transpose(2, 1, 0, 3).reshape(4096)
     n_qkv = n_all[:, :, 0:384].reshape(8, 8, 3, 128).transpose(1, 2, 0, 3).reshape(8, 3072)
-    n_fc1 = n_all[:, :, 384:896].transpose(1, 0, 2).reshape(8, 4096)
+    n_fc1 = n_all[:, :, 384:896].reshape(8, 8, 4, 4, 32).transpose(1, 3, 2, 0, 4).reshape(8, 4096)
 
     def norm_grads(weight, n, s, gain, bias_of):
         weight = weight.astype(F32)
@@ -698,7 +757,7 @@
     grad_b_fc1 = lax.dynamic_slice(sum_fc1, (me * 32,), (32,))
     grad_b_out = lax.dynamic_slice(sums[0, 1], (me * 8,), (8,))
     return (out, grad_tokens, g1_gain, g1_bias, g2_gain, g2_bias, grad_qkv, grad_b_qkv,
-            grad_b[0:8], grad_b_out, grad_fc1, grad_b_fc1, grad_b[8:40], grad_b_out)
+            grad_dense, grad_b_out, grad_fc1, grad_b_fc1, grad_fc2, grad_b_out)
 
 
 def solution(mesh):

time: 146 us -> 123 us (0.84)
  the two profiles are of different devices: /device:TPU:6 before, /device:TPU:1 now
where the time goes in v3:
time: 123 us
  Pallas kernels  107 us (87%)
  local copies, waits for them, and re-layouts  8.44 us (7%)
  other arithmetic  6.43 us (5%)
    pallas_call x1, Pallas kernels, whole(): pl.pallas_call(whole_kernel, out_shape=(jax.ShapeDtypeStruct((256, 1024),...  107 us
    unnamed x44, local copies, waits for them, and re-layouts  5.29 us
    reduce_sum x2, other arithmetic, norm_grads(): return (jnp.sum(weight * n, 1), jnp.sum(weight * s, 1), grad_w)  2.77 us

profile of v3, /device:TPU:1, one launch (start us, length us, event | category | flops | bytes accessed | tf_op | source)
XLA Modules:
  0.0 122.9 jit_solution(877312457355252280)
XLA Ops:
  0.6 0.7 convert_element_type.65
  1.3 0.0 copy-start.17
  1.4 0.0 copy-start.11
  1.4 0.0 copy-start.12
  1.4 0.0 copy-start.13
  1.4 0.6 copy-done.18
  2.0 0.0 copy-done.14
  2.0 0.0 copy-done.15
  2.0 0.0 copy-done.16
  2.0 0.0 copy-done.17
  2.0 0.0 copy-done.11
  2.1 0.0 copy-done.12
  2.1 0.0 copy-done.13
  2.1 0.7 pad_add_fusion.small_ref
  2.8 107.1 %whole_block.1 = (f32[256,1024]{1,0:T(8,128)}, f32[256,1024]{1,0:T(8,128)}, f32[8,8,896]{2,1,0:T(8,128)}, f32[8,1024]{1,0:T(8,128)}, f32[32,1024]{1,0:T(8,128)},...) custom-call(bf16[256,1024]{1,0:T(8,128)(2,1)} %x_ref.1, bf16[256,1024]{1,0:T(8,128)(2,1)} %dy_ref.1, bf16[8,3072]{1,0:T(8,128)(2,1)} %wqkv_ref.1, ...), custom_call_target="tpu_custom_call" | custom-call | flops 20000000000 | bytes 5000000 | tf_op jit(solution)/shard_map/whole_block/pallas_call | solution.py:698
  109.9 0.0 copy-start.1
  109.9 0.0 copy-done
  109.9 0.1 convert_reduce_fusion
  110.1 0.3 fusion.9
  110.4 0.8 copy-done.1
  111.1 0.4 fusion.16
  111.5 0.8 slice.18
  112.3 0.7 copy-done.10
  113.0 0.0 copy-done.2
  113.0 0.0 copy-done.3
  113.0 0.0 copy-start.6
  113.0 1.5 %fusion.8 = (bf16[256,1024]{1,0:T(8,128)(2,1)}, bf16[256,1024]{1,0:T(8,128)(2,1)}) fusion(bf16[256,1024]{1,0:T(8,128)(2,1)S(1)} %copy-done, f32[256,1024]{1,0:T(8,128)S(1)} %copy-done.1, bf16[256,1024]{1,0:T(8,128)(2,1)S(1)} %copy-done.3, f32[256]{0:T(256)S(1)} %get-tuple-element.38, f32[256]{0:T(256)S(1)} %add_rsqrt_fusion, ...), kind=kLoop, calls=%fused_computation.11 | loop fusion | flops 3670016 | bytes 4203520 | tf_op jit(solution)/shard_map/convert_element_type | solution.py:741
  114.5 0.0 copy-done.6
  114.5 0.0 copy-start.4
  114.6 0.1 reshape_squeeze.7
  114.7 0.1 mul.123
  114.8 0.6 dynamic_slice.14
  115.4 0.6 dynamic_slice.11
  116.0 0.1 dynamic-slice_bitcast_fusion
  116.1 0.0 copy-done.4
  116.1 0.3 reshape.89
  116.3 0.3 copy.34
  116.7 0.0 copy-start.7
  116.7 0.2 reshape.90
  116.9 0.6 copy-done.7
  117.5 1.4 %fusion.12 = (f32[8]{0:T(128)}, f32[8]{0:T(128)}, f32[8,4096]{1,0:T(8,128)}) fusion(bf16[8,4096]{1,0:T(8,128)(2,1)S(1)} %copy-done.7, f32[4096]{0:T(1024)S(1)} %mul.123, f32[8,4096]{1,0:T(8,128)S(1)} %reshape.90, f32[8]{0:T(128)S(1)} %convert_element_type.74, f32[8]{0:T(128)S(1)} %convert_element_type.73), kind=kLoop, calls=%fused_computation.17 | loop fusion | flops 262128 | bytes 344192 | tf_op jit(solution)/shard_map/reduce_sum | solution.py:752
  119.0 0.8 copy-done.8
  119.7 1.4 %fusion.14 = (f32[8]{0:T(128)}, f32[8]{0:T(128)}, f32[8,3072]{1,0:T(8,128)}) fusion(bf16[8,3072]{1,0:T(8,128)(2,1)S(1)} %copy-done.8, f32[3072]{0:T(1024)S(1)} %bitcast.37, f32[8,3072]{1,0:T(8,128)S(1)} %bitcast.34, f32[8]{0:T(128)S(1)} %convert_element_type.72, f32[8]{0:T(128)S(1)} %convert_element_type.71), kind=kLoop, calls=%fused_computation.22 | loop fusion | flops 196592 | bytes 258176 | tf_op jit(solution)/shard_map/reduce_sum | solution.py:752
  121.1 0.0 copy-done.19
  121.1 0.5 copy.44
  121.6 0.0 copy-done.9
  121.6 0.6 copy.45
  122.2 0.7 copy.46
  (30 shorter events, 0.2 us)
Async XLA Ops:
  1.3 0.7 copy-start.18
  1.3 0.7 copy-start.14
  1.3 0.7 copy-start.15
  1.3 0.7 copy-start.16
  1.3 0.7 copy-start.17
  1.4 0.7 copy-start.11
  1.4 0.7 copy-start.12
  1.4 0.7 copy-start.13
  2.8 107.2 %copy-start = (bf16[256,1024]{1,0:T(8,128)(2,1)S(1)}, bf16[256,1024]{1,0:T(8,128)(2,1)}, u32[]{:S(2)}) copy-start(bf16[256,1024]{1,0:T(8,128)(2,1)} %x_ref.1) | copy-start | bytes 1572868
  109.9 1.2 copy-start.1
  110.1 2.9 %copy-start.2 = (f32[256,1024]{1,0:T(8,128)S(1)}, f32[256,1024]{1,0:T(8,128)}, u32[]{:S(2)}) copy-start(f32[256,1024]{1,0:T(8,128)} %get-tuple-element.21) | copy-start | bytes 3145732
  111.1 1.8 %copy-start.3 = (bf16[256,1024]{1,0:T(8,128)(2,1)S(1)}, bf16[256,1024]{1,0:T(8,128)(2,1)}, u32[]{:S(2)}) copy-start(bf16[256,1024]{1,0:T(8,128)(2,1)} %dy_ref.1) | copy-start | bytes 1572868
  112.3 0.7 copy-start.10
  113.0 1.5 %copy-start.6 = (f32[8,8,256]{2,1,0:T(8,128)S(1)}, f32[8,8,256]{2,1,0:T(8,128)}, u32[]{:S(2)}) copy-start(f32[8,8,256]{2,1,0:T(8,128)} %get-tuple-element.25) | copy-start | bytes 196612
  114.5 1.6 %copy-start.4 = (f32[8,8,896]{2,1,0:T(8,128)S(1)}, f32[8,8,896]{2,1,0:T(8,128)}, u32[]{:S(2)}) copy-start(f32[8,8,896]{2,1,0:T(8,128)} %get-tuple-element.24) | copy-start | bytes 688132
  116.1 5.0 %copy-start.19 = (f32[8]{0:T(128)}, f32[8]{0:T(128)S(1)}, u32[]{:S(2)}) copy-start(f32[8]{0:T(128)S(1)} %dynamic-slice_bitcast_fusion) | copy-start | bytes 100
  116.7 0.8 copy-start.7
  118.9 0.8 copy-start.8
  119.7 1.9 %copy-start.9 = (f32[8,1024]{1,0:T(8,128)S(1)}, f32[8,1024]{1,0:T(8,128)}, u32[]{:S(2)}) copy-start(f32[8,1024]{1,0:T(8,128)} %get-tuple-element.90) | copy-start | bytes 98308
  119.7 2.5 %copy-start.5 = (f32[32,1024]{1,0:T(8,128)S(1)}, f32[32,1024]{1,0:T(8,128)}, u32[]{:S(2)}) copy-start(f32[32,1024]{1,0:T(8,128)} %get-tuple-element.94) | copy-start | bytes 393220

commit v4 on v3

--- a/solution.py
+++ b/solution.py
@@ -159,70 +159,67 @@
     a1 = (normed * g1 + ln_ref[1:2, :]).astype(BF)
     a2 = (normed * g2 + ln_ref[3:4, :]).astype(BF)
     joined = dot(a1, w1_ref[:, 0:384]) + bias_ref[0:1, 0:384]
-    hidden = dot(a2, w1_ref[:, 384:896]) + bias_ref[0:1, 384:896]
-    phi_cdf = 0.5 + 0.5 * lax.erf(hidden * math.sqrt(0.5))
-    active = hidden * phi_cdf
-    slope = phi_cdf + hidden * (jnp.exp(hidden * hidden * -0.5) * (1.0 / math.sqrt(2.0 * math.pi)))
 
     row = lax.broadcasted_iota(jnp.int32, (128, 128), 0)
     col = lax.broadcasted_iota(jnp.int32, (128, 128), 1)
+    low_lanes = (col & 63) < 8
+    head0 = col < 64
+    ones = jnp.ones((128, 128), BF)
+    blocks = range(2)
+    parts = [slice(b * 128, b * 128 + 128) for b in blocks]
+
+    def stacked(u):
+        zero = jnp.zeros_like(u)
+        return jnp.concatenate([jnp.where(head0, u, zero), jnp.where(head0, zero, u)], 0)
+
+    def folded(u):
+        return jnp.where(head0, u[0:128], u[128:256])
+
     masks, lives, tables = [], [], []
-    for b in range(2):
+    for b in blocks:
         seg_c = jnp.broadcast_to(seg[b : b + 1, :], (128, 128))
         seg_r = seg_c.T
         allowed = (seg_c == seg_r) & (col <= row)
         position = jnp.sum(allowed.astype(F32), 1, keepdims=True) - 1.0
         onehot = (col == position.astype(jnp.int32)).astype(BF)
         tables.append(dot(onehot, table_ref[...]))
-        masks.append(allowed)
+        masks.append(jnp.concatenate([allowed, allowed], 0))
         lives.append((seg_r[:, 0:1] >= 0.0).astype(F32))
     live = jnp.concatenate(lives, 0)
+    cosine = [u[:, 0:128] + u[:, 128:256] for u in tables]
+    sine = [u[:, 256:384] + u[:, 384:512] for u in tables]
+    q = [turn(joined[parts[b], 0:128], cosine[b], sine[b], low_lanes).astype(BF) for b in blocks]
+    k = [turn(joined[parts[b], 128:256], cosine[b], sine[b], low_lanes).astype(BF) for b in blocks]
+    v = [joined[parts[b], 256:384].astype(BF) for b in blocks]
+    q2 = [stacked(u) for u in q]
+    scores = [jnp.where(masks[b], dot_nt(q2[b], k[b]) * 0.125, MASKED) for b in blocks]
     d_cat = dot_nt(dy, w2_ref[...]) * live
+    e = [jnp.exp(u - jnp.max(u, 1, keepdims=True)) for u in scores]
+    hidden = dot(a2, w1_ref[:, 384:896]) + bias_ref[0:1, 384:896]
+    weighted = [dot(e[b].astype(BF), jnp.concatenate([v[b], ones], 1)) for b in blocks]
+    d_context = d_cat[:, 0:128].astype(BF)
+    dc2 = [stacked(d_context[p]) for p in parts]
+    d_probs = [dot_nt(dc2[b], v[b]) for b in blocks]
+    inverse = [1.0 / u[:, 128:256] for u in weighted]
+    probs = [e[b] * inverse[b] for b in blocks]
+    along = [jnp.sum(probs[b] * d_probs[b], 1, keepdims=True) for b in blocks]
+    phi_cdf = 0.5 + 0.5 * lax.erf(hidden * math.sqrt(0.5))
+    active = ((hidden * phi_cdf).astype(BF).astype(F32) * live).astype(BF)
+    slope = phi_cdf + hidden * (jnp.exp(hidden * hidden * -0.5) * (1.0 / math.sqrt(2.0 * math.pi)))
     d_hidden = d_cat[:, 128:640] * slope
-    d_context = d_cat[:, 0:128].astype(BF)
-    active = (active.astype(BF).astype(F32) * live).astype(BF)
-
-    lane = lax.broadcasted_iota(jnp.int32, (128, 128), 1)
-    low_lanes = (lane & 63) < 8
-    head0 = lane < 64
-
-    def stacked(u):
-        zero = jnp.zeros_like(u)
-        return jnp.concatenate([jnp.where(head0, u, zero), jnp.where(head0, zero, u)], 0)
-
-    ones = jnp.ones((128, 128), BF)
-    contexts, d_joined = [], []
-    for b in range(2):
-        part = slice(b * 128, b * 128 + 128)
-        cosine = tables[b][:, 0:128] + tables[b][:, 128:256]
-        sine = tables[b][:, 256:384] + tables[b][:, 384:512]
-        q = turn(joined[part, 0:128], cosine, sine, low_lanes).astype(BF)
-        k = turn(joined[part, 128:256], cosine, sine, low_lanes).astype(BF)
-        v = joined[part, 256:384].astype(BF)
-        q2 = stacked(q)
-        allowed = jnp.concatenate([masks[b], masks[b]], 0)
-        scores = jnp.where(allowed, dot_nt(q2, k) * 0.125, MASKED)
-        e = jnp.exp(scores - jnp.max(scores, 1, keepdims=True))
-        ctx = dot(e.astype(BF), jnp.concatenate([v, ones], 1))
-        inverse = 1.0 / ctx[:, 128:256]
-        probs = e * inverse
-        probs_b = probs.astype(BF)
-        ctx = ctx[:, 0:128] * inverse
-        ctx = jnp.where(head0, ctx[0:128], ctx[128:256]).astype(BF).astype(F32)
-        contexts.append((ctx * lives[b]).astype(BF))
-        dc2 = stacked(d_context[part])
-        d_probs = dot_nt(dc2, v)
-        d_v = dot_tn(probs_b, dc2)
-        d_scores = probs * (d_probs - jnp.sum(probs * d_probs, 1, keepdims=True))
-        d_scores = d_scores.astype(BF)
-        dq2 = dot(d_scores, k) * 0.125
-        d_q = jnp.where(head0, dq2[0:128], dq2[128:256])
-        d_k = dot_tn(d_scores, q2) * 0.125
-        d_joined.append(
-            jnp.concatenate(
-                [turn(d_q, cosine, -sine, low_lanes), turn(d_k, cosine, -sine, low_lanes), d_v], 1
-            )
+    d_scores = [(probs[b] * (d_probs[b] - along[b])).astype(BF) for b in blocks]
+    contexts = [
+        (folded(weighted[b][:, 0:128] * inverse[b]).astype(BF).astype(F32) * lives[b]).astype(BF) for b in blocks
+    ]
+    d_v = [dot_tn(probs[b].astype(BF), dc2[b]) for b in blocks]
+    d_q = [folded(dot(d_scores[b], k[b]) * 0.125) for b in blocks]
+    d_k = [dot_tn(d_scores[b], q2[b]) * 0.125 for b in blocks]
+    d_joined = [
+        jnp.concatenate(
+            [turn(d_q[b], cosine[b], -sine[b], low_lanes), turn(d_k[b], cosine[b], -sine[b], low_lanes), d_v[b]], 1
         )
+        for b in blocks
+    ]
     cat = jnp.concatenate([jnp.concatenate(contexts, 0), active], 1)
     out = dot(cat, w2_ref[...])
     d_all = jnp.concatenate([jnp.concatenate(d_joined, 0), d_hidden], 1)
@@ -441,10 +438,10 @@
         ref = dst.at[mine(ring_y.bwd)]
         msgs.send((name, 3), ref, ref, y_dev(ring_y.fwd))
 
-    rows_on("x", X)
     for sub in ("bwd", "fwd", "opp"):
         for h in halves:
             pass_on(h, sub)
+    rows_on("x", X)
     rows_on("d", DY)
     rows_far("x", X)
     rows_far("d", DY)
@@ -471,7 +468,7 @@
 
     OUT, G, NB, DALL, CAT, sib, from_y = (m[k] for k in ("OUT", "G", "NB", "DALL", "CAT", "sib", "from_y"))
     arrays = ((0, OUT, out_sum), (1, G, g_sum))
-    chips = [lax.rem(y + k, 4) for k in (3, 1, 2, 0)]
+    chips = [lax.rem(y + k, 4) for k in (0, 3, 1, 2)]
 
     def join(a, src, at, extra=None):
         def add(r):
@@ -495,24 +492,24 @@
         @pl.when(s == 0)
         def _():
             for name in "xd":
+                msgs.land((name, 2))
+
+        @pl.when(s == 2)
+        def _():
+            for name in "xd":
                 msgs.land((name, 4))
                 msgs.land((name, 5))
 
-        @pl.when(s == 2)
+        @pl.when(s == 4)
         def _():
             for name in "xd":
                 msgs.land((name, 3))
                 msgs.sent[name, 6].start()
 
-        @pl.when(s == 4)
-        def _():
-            msgs.land(("x", 6))
-            msgs.land(("d", 6))
-
         @pl.when(s == 6)
         def _():
-            msgs.land(("x", 2))
-            msgs.land(("d", 2))
+            for name in "xd":
+                msgs.land((name, 6))
 
     def after(s):
         for k in range(4):
@@ -522,20 +519,13 @@
                 for a, src, _ in arrays:
                     msgs.sent["sib", a, k].start()
 
-        @pl.when(s == 3)
-        def _():
-            for a, src, _ in arrays:
-                msgs.land(("sib", a, 0))
-                msgs.land(("sib", a, 1))
-                join(a, src, ring_y.bwd)
-                msgs.sent["y", a, 1].start()
-
         @pl.when(s == 5)
         def _():
             for a, src, _ in arrays:
+                msgs.land(("sib", a, 1))
                 msgs.land(("sib", a, 2))
-                join(a, src, ring_y.opp)
-                msgs.sent["y", a, 0].start()
+                join(a, src, ring_y.bwd)
+                msgs.sent["y", a, 1].start()
 
     def one_slot(s, carry):
         before(s)
@@ -617,27 +607,32 @@
         msgs.land((h.name, "two", 2))
         return v + into_two[h.name][1].astype(F32) + into_two[h.name][2].astype(F32)
 
+    grad_a(ring_x.opp)
+    send_one(ha, 0, ring_x.opp, ring_x.fwd)
+
+    for a, src, _ in arrays:
+        msgs.land(("sib", a, 3))
+        join(a, src, ring_y.opp)
+        msgs.sent["y", a, 0].start()
+
+    grad_a(ring_x.bwd)
+    send_one(ha, 1, ring_x.bwd, ring_x.bwd)
     v = dot_tn(CAT[:, :, 0:128].reshape(2048, 128), DY[...].reshape(2048, 1024)).reshape(4, 4, 8, 1024)
     part["b"][:, :, 0:16, :] = jnp.concatenate([v, jnp.zeros_like(v)], 2).astype(BF)
-    grad_a(ring_x.opp)
-    send_one(ha, 0, ring_x.opp, ring_x.fwd)
     grad_b(ring_z.opp, ring_z.bwd)
     send_one(hb, 0, ring_z.opp, ring_z.fwd)
     send_one(hb, 1, ring_z.bwd, ring_z.bwd)
-
-    for a, src, _ in arrays:
-        msgs.land(("y", a, 0))
-        join(a, src, ring_y.fwd, extra=0)
-        msgs.send(("y", a, 2), src.at[mine(ring_y.fwd)], from_y.at[a, 2], y_dev(ring_y.fwd))
-
-    grad_a(ring_x.bwd)
-    send_one(ha, 1, ring_x.bwd, ring_x.bwd)
     grad_a(ring_x.fwd)
     for sub in subs:
         send_forward(ha, sub)
     grad_b(ring_z.fwd, ring_z.own)
     for sub in subs:
         send_forward(hb, sub)
+
+    for a, src, _ in arrays:
+        msgs.land(("y", a, 0))
+        join(a, src, ring_y.fwd, extra=0)
+        msgs.send(("y", a, 2), src.at[mine(ring_y.fwd)], from_y.at[a, 2], y_dev(ring_y.fwd))
     grad_a(ring_x.own)
 
     for k in range(3):
@@ -659,35 +654,39 @@
     for h in halves:
         first_sum(h, "fwd")
 
-    for a, src, dst in arrays:
-        msgs.land(("sib", a, 3))
-        msgs.land(("y", a, 1))
-        msgs.land(("y", a, 2))
-
-        def add(r, a=a, src=src, dst=dst):
-            v = src[mine(y), r, :].astype(F32) + sib[a, y, r, :].astype(F32)
-            dst[r, :] = v + from_y[a, 1, r, :].astype(F32) + from_y[a, 2, r, :].astype(F32)
-
-        slabs(256, 32, add)
+    v = first_sum(hb, "own")
+    m["own_dense"][...] = v[0:8]
+    grad_fc2[...] = v[16:48]
+
+    @pl.when(moves)
+    def _():
+        msgs.sent["back"].start()
+
+    @pl.when(jnp.logical_not(moves))
+    def _():
+        grad_dense[...] = m["own_dense"][...]
 
     fin_a = m["fin_a"]
     fin_a[...] = first_sum(ha, "own").reshape(8, 8, 896)
     for k, o in enumerate(others):
         msgs.send(("n", k), fin_a.at[o], n_all.at[t], group_member(x, z, o))
     n_all[t] = fin_a[t]
-    v = first_sum(hb, "own")
-    m["own_dense"][...] = v[0:8]
-    grad_fc2[...] = v[16:48]
+
+    for a, src, dst in arrays:
+        msgs.land(("sib", a, 0))
+        msgs.land(("y", a, 1))
+        msgs.land(("y", a, 2))
+
+        def add(r, a=a, src=src, dst=dst):
+            v = src[mine(y), r, :].astype(F32) + sib[a, y, r, :].astype(F32)
+            dst[r, :] = v + from_y[a, 1, r, :].astype(F32) + from_y[a, 2, r, :].astype(F32)
+
+        slabs(256, 32, add)
 
     @pl.when(moves)
     def _():
-        msgs.sent["back"].start()
         msgs.sent["there"].wait_send()
         msgs.sent["back"].wait()
-
-    @pl.when(jnp.logical_not(moves))
-    def _():
-        grad_dense[...] = m["own_dense"][...]
 
     msgs.finish()
 
@@ -718,10 +717,94 @@
     )(*args)
 
 
+def finish_kernel(*refs):
+    given, results, held, sems = refs[:12], refs[12:26], refs[26:38], refs[38]
+    copies = [pltpu.make_async_copy(src, dst, sems.at[n]) for n, (src, dst) in enumerate(zip(given, held))]
+    for copy in copies:
+        copy.start()
+    for copy in copies:
+        copy.wait()
+    x_ref, dy_ref, out_sum, g_sum, n_all, dense_in, fc2_in, vec_all, b_out, small_ref, wqkv_ref, wfc1_ref = held
+    (out_ref, dx_ref, g1_gain, g1_bias, g2_gain, g2_bias, grad_qkv, grad_b_qkv,
+     grad_dense, grad_b_out, grad_fc1, grad_b_fc1, grad_fc2, grad_b_last) = results
+    me = lax.axis_index("fsdp")
+    small = small_ref[...].astype(F32)
+    lives = [jnp.broadcast_to(small[b : b + 1, :], (128, 128)).T[:, 0:1] >= 0.0 for b in (1, 2)]
+    live = jnp.concatenate([u.astype(F32) for u in lives], 0)
+    x = x_ref[...].astype(F32)
+    out_ref[...] = (x + live * (out_sum[...] + b_out[0:1, :])).astype(BF)
+    centre = x - jnp.mean(x, 1, keepdims=True)
+    scale = lax.rsqrt(jnp.mean(centre * centre, 1, keepdims=True) + NORM_EPS)
+    normed = centre * scale
+    g = g_sum[...]
+    dx = (g - jnp.mean(g, 1, keepdims=True) - normed * jnp.mean(g * normed, 1, keepdims=True)) * scale
+    dx_ref[...] = (dy_ref[...].astype(F32) + dx).astype(BF)
+
+    row = lax.broadcasted_iota(jnp.int32, (8, 128), 0)
+    lane = lax.broadcasted_iota(jnp.int32, (8, 128), 1)
+
+    def column(start):
+        return jnp.sum(jnp.where(lane == row + start, small[0:1, :], 0.0), 1, keepdims=True)
+
+    def as_lanes(u):
+        return jnp.sum(jnp.where(lane == row, u, 0.0), 0, keepdims=True)
+
+    def write(ref, u, count):
+        ref[...] = u[0:1, 0:count]
+
+    def shifted(u, by):
+        width = u.shape[1]
+        return pltpu.roll(jnp.broadcast_to(u, (8, width)), lax.rem(width - by, width), 1)
+
+    n_qkv = jnp.concatenate([n_all[t, :, c * 128 : c * 128 + 128] for c in range(3) for t in range(8)], 1)
+    at = ((0, 0), (0, 128), (1, 0))
+    s_qkv = jnp.concatenate([vec_all[t, r : r + 1, lo : lo + 128] for r, lo in at for t in range(8)], 1)
+    both = []
+    for t in range(8):
+        sums = jnp.concatenate([vec_all[t, 1:2, 128:256], vec_all[t, 2:3, :], vec_all[t, 3:4, 0:128]], 1)
+        both.append(jnp.concatenate([n_all[t, :, 384:896], jnp.broadcast_to(sums, (8, 512))], 0))
+    fc1 = jnp.concatenate(
+        [both[t][:, (q * 4 + p) * 32 : (q * 4 + p) * 32 + 32] for p in range(4) for q in range(4) for t in range(8)], 1
+    )
+
+    def norm_grads(weight, n, s, start, gain_ref, bias_ref, grad_ref):
+        weight = weight.astype(F32)
+        grad_ref[...] = column(start) * n + column(start + 8) * s
+        write(gain_ref, as_lanes(jnp.sum(weight * n, 1, keepdims=True)), 8)
+        write(bias_ref, as_lanes(jnp.sum(weight * s, 1, keepdims=True)), 8)
+
+    s_fc1 = fc1[8:9]
+    norm_grads(wqkv_ref[...], n_qkv, s_qkv, 0, g1_gain, g1_bias, grad_qkv)
+    norm_grads(wfc1_ref[...], fc1[0:8], s_fc1, 16, g2_gain, g2_bias, grad_fc1)
+    write(grad_b_qkv, shifted(s_qkv, me * 24), 24)
+    write(grad_b_fc1, shifted(s_fc1, me * 32), 32)
+    branch = jnp.concatenate([vec_all[0, r : r + 1, :] for r in range(4, 8)], 1)
+    branch = shifted(branch, me * 8)
+    write(grad_b_out, branch, 8)
+    write(grad_b_last, branch, 8)
+    grad_dense[...] = dense_in[...]
+    grad_fc2[...] = fc2_in[...]
+
+
+def finish(*args):
+    flat = lambda count: jax.ShapeDtypeStruct((1, count), F32)
+    full = lambda *shape: jax.ShapeDtypeStruct(shape, F32)
+    rows = jax.ShapeDtypeStruct((256, 1024), BF)
+    outs = pl.pallas_call(
+        finish_kernel,
+        out_shape=(rows, rows, flat(8), flat(8), flat(8), flat(8), full(8, 3072), flat(24), full(8, 1024), flat(8),
+                   full(8, 4096), flat(32), full(32, 1024), flat(8)),
+        in_specs=[pl.BlockSpec(memory_space=pl.ANY)] * len(args),
+        scratch_shapes=[pltpu.VMEM(u.shape, u.dtype) for u in args] + [pltpu.SemaphoreType.DMA((len(args),))],
+        compiler_params=pltpu.CompilerParams(vmem_limit_bytes=VMEM_LIMIT),
+        cost_estimate=pl.CostEstimate(flops=20_000_000, bytes_accessed=6_000_000, transcendentals=0),
+        name="finish",
+    )(*args)
+    return tuple(u.reshape(-1) if u.shape[0] == 1 else u for u in outs)
+
+
 def body(tokens, segments, grad_out, ln1_gain, ln1_bias, ln2_gain, ln2_bias, w_qkv, b_qkv,
          w_dense, b_dense, w_fc1, b_fc1, w_fc2, b_fc2):
-    me = lax.axis_index("fsdp")
-
     small = jnp.pad(segments.astype(BF), ((1, 5), (0, 0)))
     at = 0
     for vector in (ln1_gain, ln1_bias, ln2_gain, ln2_bias, b_qkv, b_fc1, b_dense, b_fc2):
@@ -731,33 +814,9 @@
         tokens, grad_out, w_qkv, w_fc1, w_dense, w_fc2, small, jnp.asarray(rotary_table())
     )
 
-    live = (segments.reshape(256, 1) >= 0).astype(F32)
-    x = tokens.astype(F32)
-    out = (x + live * (out_sum + b_out[0:1, :])).astype(BF)
-    centre = x - jnp.mean(x, -1, keepdims=True)
-    scale = lax.rsqrt(jnp.mean(centre * centre, -1, keepdims=True) + NORM_EPS)
-    normed = centre * scale
-    dx = (g_sum - jnp.mean(g_sum, -1, keepdims=True) - normed * jnp.mean(g_sum * normed, -1, keepdims=True)) * scale
-    grad_tokens = (grad_out.astype(F32) + dx).astype(BF)
-
-    sums = sums.reshape(8, 2, 1024)
-    sum_qkv = sums[:, 0, 0:384].reshape(8, 3, 128).transpose(1, 0, 2).reshape(3072)
-    sum_fc1 = sums[:, 0, 384:896].reshape(8, 4, 4, 32).transpose(2, 1, 0, 3).reshape(4096)
-    n_qkv = n_all[:, :, 0:384].reshape(8, 8, 3, 128).transpose(1, 2, 0, 3).reshape(8, 3072)
-    n_fc1 = n_all[:, :, 384:896].reshape(8, 8, 4, 4, 32).transpose(1, 3, 2, 0, 4).reshape(8, 4096)
-
-    def norm_grads(weight, n, s, gain, bias_of):
-        weight = weight.astype(F32)
-        grad_w = gain.astype(F32)[:, None] * n + bias_of.astype(F32)[:, None] * s
-        return jnp.sum(weight * n, 1), jnp.sum(weight * s, 1), grad_w
-
-    g1_gain, g1_bias, grad_qkv = norm_grads(w_qkv, n_qkv, sum_qkv, ln1_gain, ln1_bias)
-    g2_gain, g2_bias, grad_fc1 = norm_grads(w_fc1, n_fc1, sum_fc1, ln2_gain, ln2_bias)
-    grad_b_qkv = lax.dynamic_slice(sum_qkv, (me * 24,), (24,))
-    grad_b_fc1 = lax.dynamic_slice(sum_fc1, (me * 32,), (32,))
-    grad_b_out = lax.dynamic_slice(sums[0, 1], (me * 8,), (8,))
-    return (out, grad_tokens, g1_gain, g1_bias, g2_gain, g2_bias, grad_qkv, grad_b_qkv,
-            grad_dense, grad_b_out, grad_fc1, grad_b_fc1, grad_fc2, grad_b_out)
+    return finish(
+        tokens, grad_out, out_sum, g_sum, n_all, grad_dense, grad_fc2, sums, b_out, small, w_qkv, w_fc1
+    )
 
 
 def solution(mesh):

time: 123 us -> 106 us (0.86)
  local copies, waits for them, and re-layouts: 8.44 us -> 1.27 us
  other arithmetic: 6.43 us -> 0.67 us
  Pallas kernels: 107 us -> 103 us
    pallas_call x1, Pallas kernels: 107 us -> 99 us  [whole(): pl.pallas_call(whole_kernel, out_shape=(jax.ShapeDtypeStruct((256, 1024),...]
    pallas_call x0 -> x1, Pallas kernels: none -> 4.1 us  [finish(): pl.pallas_call(finish_kernel, out_shape=(rows, rows, flat(8), flat(8), fl...]
    unnamed x44 -> x18, local copies, waits for them, and re-layouts: 5.29 us -> 1.27 us
    reduce_sum x5 -> x0, other arithmetic: 3.56 us -> none  [the longest x2 2.77 us: norm_grads(): return (jnp.sum(weight * n, 1), jnp.sum(weight * s, 1), grad_w)]
    convert_element_type x6 -> x0, other arithmetic: 1.5 us -> none  [the longest x1 1.48 us: body(): grad_tokens = (grad_out.astype(F32) + dx).astype(BF)]
    dynamic_slice x3 -> x0, local copies, waits for them, and re-layouts: 1.25 us -> none  [the longest x1 0.59 us: body(): grad_b_qkv = lax.dynamic_slice(sum_qkv, (me * 24,), (24,))]
where the time goes in v4:
time: 106 us
  Pallas kernels  103 us (97%)
  local copies, waits for them, and re-layouts  1.27 us (1%)
    pallas_call x1, Pallas kernels, whole(): pl.pallas_call(whole_kernel, out_shape=(jax.ShapeDtypeStruct((256, 1024),...  99 us
    pallas_call x1, Pallas kernels, finish(): pl.pallas_call(finish_kernel, out_shape=(rows, rows, flat(8), flat(8), fl...  4.1 us

profile of v4, /device:TPU:1, one launch (start us, length us, event | category | flops | bytes accessed | tf_op | source)
XLA Modules:
  0.0 105.8 jit_solution(4121930061391129598)
XLA Ops:
  0.6 0.0 copy-start.8
  0.7 0.0 copy-start.7
  0.7 0.0 copy-start.3
  0.7 0.0 copy-start.4
  0.7 0.0 copy-start.5
  0.7 0.0 copy-start.6
  0.7 0.6 copy-done.8
  1.3 0.0 copy-start
  1.3 0.0 copy-start.1
  1.3 0.0 copy-start.2
  1.3 0.0 copy-done.7
  1.4 0.0 copy-done.3
  1.4 0.0 copy-done.4
  1.4 0.0 copy-done.5
  1.4 0.0 copy-done.6
  1.4 0.6 copy-done
  2.0 0.0 copy-done.1
  2.0 0.0 copy-done.2
  2.0 0.7 pad_add_fusion.small_ref.refs_9_
  2.7 99.0 %whole_block.1 = (f32[256,1024]{1,0:T(8,128)}, f32[256,1024]{1,0:T(8,128)}, f32[8,8,896]{2,1,0:T(8,128)}, f32[8,1024]{1,0:T(8,128)}, f32[32,1024]{1,0:T(8,128)},...) custom-call(bf16[256,1024]{1,0:T(8,128)(2,1)} %refs_0_.1, bf16[256,1024]{1,0:T(8,128)(2,1)} %refs_1_.1, ...), custom_call_target="tpu_custom_call" | custom-call | flops 20000000000 | bytes 5000000 | tf_op jit(solution)/shard_map/whole_block/pallas_call | solution.py:697
  101.7 4.1 %finish.1 = (bf16[256,1024]{1,0:T(8,128)(2,1)}, bf16[256,1024]{1,0:T(8,128)(2,1)}, f32[1,8]{1,0:T(1,128)}, f32[1,8]{1,0:T(1,128)}, f32[1,8]{1,0:T(1,128)}, /*ind...) custom-call(bf16[256,1024]{1,0:T(8,128)(2,1)} %refs_0_.1, ...), custom_call_target="tpu_custom_call" | custom-call | flops 20000000 | bytes 6000000 | tf_op jit(solution)/shard_map/finish/pallas_call | solution.py:793
  (1 shorter events, 0.0 us)
Async XLA Ops:
  0.6 0.7 copy-start.8
  0.7 0.7 copy-start.7
  0.7 0.7 copy-start.3
  0.7 0.7 copy-start.4
  0.7 0.7 copy-start.5
  0.7 0.7 copy-start.6
  1.3 0.7 copy-start
  1.3 0.7 copy-start.1
  1.3 0.7 copy-start.2

commit v5 on v4

--- a/solution.py
+++ b/solution.py
@@ -500,7 +500,7 @@
                 msgs.land((name, 4))
                 msgs.land((name, 5))
 
-        @pl.when(s == 4)
+        @pl.when(s == 5)
         def _():
             for name in "xd":
                 msgs.land((name, 3))
@@ -722,12 +722,12 @@
     copies = [pltpu.make_async_copy(src, dst, sems.at[n]) for n, (src, dst) in enumerate(zip(given, held))]
     for copy in copies:
         copy.start()
-    for copy in copies:
-        copy.wait()
     x_ref, dy_ref, out_sum, g_sum, n_all, dense_in, fc2_in, vec_all, b_out, small_ref, wqkv_ref, wfc1_ref = held
     (out_ref, dx_ref, g1_gain, g1_bias, g2_gain, g2_bias, grad_qkv, grad_b_qkv,
      grad_dense, grad_b_out, grad_fc1, grad_b_fc1, grad_fc2, grad_b_last) = results
     me = lax.axis_index("fsdp")
+    for n in (0, 2, 8, 9):
+        copies[n].wait()
     small = small_ref[...].astype(F32)
     lives = [jnp.broadcast_to(small[b : b + 1, :], (128, 128)).T[:, 0:1] >= 0.0 for b in (1, 2)]
     live = jnp.concatenate([u.astype(F32) for u in lives], 0)
@@ -736,6 +736,8 @@
     centre = x - jnp.mean(x, 1, keepdims=True)
     scale = lax.rsqrt(jnp.mean(centre * centre, 1, keepdims=True) + NORM_EPS)
     normed = centre * scale
+    for n in (1, 3):
+        copies[n].wait()
     g = g_sum[...]
     dx = (g - jnp.mean(g, 1, keepdims=True) - normed * jnp.mean(g * normed, 1, keepdims=True)) * scale
     dx_ref[...] = (dy_ref[...].astype(F32) + dx).astype(BF)
@@ -756,6 +758,8 @@
         width = u.shape[1]
         return pltpu.roll(jnp.broadcast_to(u, (8, width)), lax.rem(width - by, width), 1)
 
+    for n in (4, 5, 6, 7, 10, 11):
+        copies[n].wait()
     n_qkv = jnp.concatenate([n_all[t, :, c * 128 : c * 128 + 128] for c in range(3) for t in range(8)], 1)
     at = ((0, 0), (0, 128), (1, 0))
     s_qkv = jnp.concatenate([vec_all[t, r : r + 1, lo : lo + 128] for r, lo in at for t in range(8)], 1)

time: 106 us -> 107 us (level)
  no operation moved by 1% of the time
where the time goes in v5:
time: 107 us; the launch traced here: 106 us
  Pallas kernels  104 us (97%)
  local copies, waits for them, and re-layouts  1.27 us (1%)
    pallas_call x1, Pallas kernels, whole(): pl.pallas_call(whole_kernel, out_shape=(jax.ShapeDtypeStruct((256, 1024),...  99.6 us
    pallas_call x1, Pallas kernels, finish(): pl.pallas_call(finish_kernel, out_shape=(rows, rows, flat(8), flat(8), fl...  4.21 us

profile of v5, /device:TPU:1, one launch (start us, length us, event | category | flops | bytes accessed | tf_op | source)
XLA Modules:
  0.0 106.5 jit_solution(12692274539614592599)
XLA Ops:
  0.6 0.0 copy-start.8
  0.7 0.0 copy-start.7
  0.7 0.0 copy-start.3
  0.7 0.0 copy-start.4
  0.7 0.0 copy-start.5
  0.7 0.0 copy-start.6
  0.7 0.6 copy-done.8
  1.3 0.0 copy-start
  1.3 0.0 copy-start.1
  1.3 0.0 copy-start.2
  1.3 0.0 copy-done.7
  1.4 0.0 copy-done.3
  1.4 0.0 copy-done.4
  1.4 0.0 copy-done.5
  1.4 0.0 copy-done.6
  1.4 0.6 copy-done
  2.0 0.0 copy-done.1
  2.0 0.0 copy-done.2
  2.0 0.7 pad_add_fusion.small_ref.refs_9_
  2.7 99.6 %whole_block.1 = (f32[256,1024]{1,0:T(8,128)}, f32[256,1024]{1,0:T(8,128)}, f32[8,8,896]{2,1,0:T(8,128)}, f32[8,1024]{1,0:T(8,128)}, f32[32,1024]{1,0:T(8,128)},...) custom-call(bf16[256,1024]{1,0:T(8,128)(2,1)} %refs_0_.1, bf16[256,1024]{1,0:T(8,128)(2,1)} %refs_1_.1, ...), custom_call_target="tpu_custom_call" | custom-call | flops 20000000000 | bytes 5000000 | tf_op jit(solution)/shard_map/whole_block/pallas_call | solution.py:697
  102.3 4.2 %finish.1 = (bf16[256,1024]{1,0:T(8,128)(2,1)}, bf16[256,1024]{1,0:T(8,128)(2,1)}, f32[1,8]{1,0:T(1,128)}, f32[1,8]{1,0:T(1,128)}, f32[1,8]{1,0:T(1,128)}, /*ind...) custom-call(bf16[256,1024]{1,0:T(8,128)(2,1)} %refs_0_.1, ...), custom_call_target="tpu_custom_call" | custom-call | flops 20000000 | bytes 6000000 | tf_op jit(solution)/shard_map/finish/pallas_call | solution.py:797
  (1 shorter events, 0.0 us)
Async XLA Ops:
  0.6 0.7 copy-start.8
  0.7 0.7 copy-start.7
  0.7 0.7 copy-start.3
  0.7 0.7 copy-start.4
  0.7 0.7 copy-start.5
  0.7 0.7 copy-start.6
  1.3 0.7 copy-start
  1.3 0.7 copy-start.1
  1.3 0.7 copy-start.2

commit v6 on v4

--- a/solution.py
+++ b/solution.py
@@ -442,8 +442,8 @@
         for h in halves:
             pass_on(h, sub)
     rows_on("x", X)
+    rows_far("x", X)
     rows_on("d", DY)
-    rows_far("x", X)
     rows_far("d", DY)
     for h in halves:
         for sub in ("own", "bwd", "fwd", "opp"):

time: 106 us -> 107 us (level)
  no operation moved by 1% of the time
where the time goes in v6:
time: 107 us; the launch traced here: 106 us
  Pallas kernels  104 us (97%)
  local copies, waits for them, and re-layouts  1.27 us (1%)
    pallas_call x1, Pallas kernels, whole(): pl.pallas_call(whole_kernel, out_shape=(jax.ShapeDtypeStruct((256, 1024),...  99.7 us
    pallas_call x1, Pallas kernels, finish(): pl.pallas_call(finish_kernel, out_shape=(rows, rows, flat(8), flat(8), fl...  4.1 us

profile of v6, /device:TPU:1, one launch (start us, length us, event | category | flops | bytes accessed | tf_op | source)
XLA Modules:
  0.0 106.4 jit_solution(10634872724206785865)
XLA Ops:
  0.6 0.0 copy-start.8
  0.7 0.0 copy-start.7
  0.7 0.0 copy-start.3
  0.7 0.0 copy-start.4
  0.7 0.0 copy-start.5
  0.7 0.0 copy-start.6
  0.7 0.6 copy-done.8
  1.3 0.0 copy-start
  1.3 0.0 copy-start.1
  1.3 0.0 copy-start.2
  1.3 0.0 copy-done.7
  1.4 0.0 copy-done.3
  1.4 0.0 copy-done.4
  1.4 0.0 copy-done.5
  1.4 0.0 copy-done.6
  1.4 0.6 copy-done
  2.0 0.0 copy-done.1
  2.0 0.0 copy-done.2
  2.0 0.7 pad_add_fusion.small_ref.refs_9_
  2.7 99.7 %whole_block.1 = (f32[256,1024]{1,0:T(8,128)}, f32[256,1024]{1,0:T(8,128)}, f32[8,8,896]{2,1,0:T(8,128)}, f32[8,1024]{1,0:T(8,128)}, f32[32,1024]{1,0:T(8,128)},...) custom-call(bf16[256,1024]{1,0:T(8,128)(2,1)} %refs_0_.1, bf16[256,1024]{1,0:T(8,128)(2,1)} %refs_1_.1, ...), custom_call_target="tpu_custom_call" | custom-call | flops 20000000000 | bytes 5000000 | tf_op jit(solution)/shard_map/whole_block/pallas_call | solution.py:697
  102.3 4.1 %finish.1 = (bf16[256,1024]{1,0:T(8,128)(2,1)}, bf16[256,1024]{1,0:T(8,128)(2,1)}, f32[1,8]{1,0:T(1,128)}, f32[1,8]{1,0:T(1,128)}, f32[1,8]{1,0:T(1,128)}, /*ind...) custom-call(bf16[256,1024]{1,0:T(8,128)(2,1)} %refs_0_.1, ...), custom_call_target="tpu_custom_call" | custom-call | flops 20000000 | bytes 6000000 | tf_op jit(solution)/shard_map/finish/pallas_call | solution.py:793
  (1 shorter events, 0.0 us)
Async XLA Ops:
  0.6 0.7 copy-start.8
  0.7 0.7 copy-start.7
  0.7 0.7 copy-start.3
  0.7 0.7 copy-start.4
  0.7 0.7 copy-start.5
  0.7 0.7 copy-start.6
  1.3 0.7 copy-start
  1.3 0.7 copy-start.1
  1.3 0.7 copy-start.2
